TPU v7x, 32 devices: a whole 2x2x4 slice. The times are simulated.
32 devices in a mesh: seq: 16 (over z, y, core), sp: 2 (over x).
Axes of the slice: x: 2, y: 2, z: 4, core: 2. Of those that a mesh axis runs over, the one named last changes fastest.
Arguments:
- frames: bfloat16 [16, 1664, 1024], P('seq', 'sp'), may hold values from -6 to 6
- clip_ids: int32 [16, 1664], P('seq'), may hold values from 0 to 7, never falling along the last dimension, each value on 1 to 350 neighbouring positions
- norm_gain: float32 [1024], replicated, may hold values from 0.5 to 1.5
- w_query: bfloat16 [1024, 1024], replicated, may hold values from -0.1875 to 0.1875
- w_key: bfloat16 [1024, 1024], replicated, may hold values from -0.1875 to 0.1875
- w_value: bfloat16 [1024, 1024], replicated, may hold values from -0.1875 to 0.1875
- w_output: bfloat16 [1024, 1024], replicated, may hold values from -0.5 to 0.5
- attn_scale: float32 [1024], replicated, may hold values from 0.5 to 1.5
- mlp_gain: float32 [1024], replicated, may hold values from 0.5 to 1.5
- w_gate: bfloat16 [1024, 4096], replicated, may hold values from -0.1875 to 0.1875
- w_up: bfloat16 [1024, 4096], replicated, may hold values from -0.1875 to 0.1875
- w_down: bfloat16 [4096, 1024], replicated, may hold values from -0.09375 to 0.09375
- mlp_scale: float32 [1024], replicated, may hold values from 0.5 to 1.5
- out_grad: bfloat16 [16, 1664, 1024], P('seq', 'sp'), may hold values from -6 to 6
Outputs:
- layer_out: bfloat16 [16, 1664, 1024], P('seq', 'sp')
- frames_grad: bfloat16 [16, 1664, 1024], P('seq', 'sp')
- norm_grad: float32 [1024], P(('seq', 'sp'))
- query_grad: float32 [1024, 1024], P(('seq', 'sp'))
- key_grad: float32 [1024, 1024], P(('seq', 'sp'))
- value_grad: float32 [1024, 1024], P(('seq', 'sp'))
- output_grad: float32 [1024, 1024], P(('seq', 'sp'))
- attn_scale_grad: float32 [1024], P(('seq', 'sp'))
- mlp_norm_grad: float32 [1024], P(('seq', 'sp'))
- gate_grad: float32 [1024, 4096], P(('seq', 'sp'))
- up_grad: float32 [1024, 4096], P(('seq', 'sp'))
- down_grad: float32 [4096, 1024], P(('seq', 'sp'))
- mlp_scale_grad: float32 [1024], P(('seq', 'sp'))
Inputs may be any that keep to these rules, and one draw needn't show every extreme that they name: `clip_ids`: clip numbers never fall along a sequence; every clip has 1 to 350 frames and one clip of each sequence has exactly 350.
All inputs are finite; a program needn't handle non-finite values.
Results may differ from a plain program's by a relative error of at most 0.014.
Values may be sent and summed in bfloat16 or wider, within the bound.
No kernel may reach another device: no remote copies, remote signals or barrier semaphores. Data moves between devices by JAX's collectives and lax.ppermute only.
A program may use at most 320 MiB of HBM per device.

v0:
```python
import math

import jax
import jax.numpy as jnp
from jax import lax
from jax.sharding import PartitionSpec as P

HEAD_DIM = 64
WINDOW = 128
BLOCK = 832


ln_eps = 1e-05
rms_eps = 1e-06


def clip_positions(clip_rows):
    last_axis = clip_rows.ndim - 1
    frame_index = lax.broadcasted_iota(jnp.int32, clip_rows.shape, last_axis)
    previous = jnp.concatenate([clip_rows[..., :1] - 1, clip_rows[..., :-1]], axis=last_axis)
    starting = jnp.where(clip_rows != previous, frame_index, jnp.zeros_like(frame_index))
    first_frame = lax.cummax(starting, axis=last_axis)
    return (frame_index - first_frame).astype(jnp.float32)


def rotary_tables(positions):
    half_dim = HEAD_DIM // 2
    exponent = jnp.arange(half_dim, dtype=jnp.float32) * (2.0 / HEAD_DIM)
    frequency = jnp.exp(-math.log(10000.0) * exponent)
    angles = positions[..., None] * frequency
    return (jnp.cos(angles), jnp.sin(angles))


def rotate(values_in, cos_tab, sin_tab):
    half_dim = values_in.shape[-1] // 2
    leading, trailing = (values_in[..., :half_dim], values_in[..., half_dim:])
    cos_use = cos_tab[..., None, :]
    sin_use = sin_tab[..., None, :]
    return jnp.concatenate(
        [leading * cos_use - trailing * sin_use, trailing * cos_use + leading * sin_use], axis=-1
    )


def rotate_back(values_in, cos_tab, sin_tab):
    half_dim = values_in.shape[-1] // 2
    leading, trailing = (values_in[..., :half_dim], values_in[..., half_dim:])
    cos_use = cos_tab[..., None, :]
    sin_use = sin_tab[..., None, :]
    return jnp.concatenate(
        [leading * cos_use + trailing * sin_use, trailing * cos_use - leading * sin_use], axis=-1
    )


def key_tiles(key_blk):
    return key_blk[:, None]


def untile_keys(grad_tiles):
    return grad_tiles[:, 0]


def band_allowed(clip_query, clip_keys, tile):
    span_keys = tile + WINDOW
    offsets = lax.broadcasted_iota(jnp.int32, (tile, span_keys), 1) - lax.broadcasted_iota(
        jnp.int32, (tile, span_keys), 0
    )
    banded = (offsets >= 0) & (offsets < WINDOW)
    return ((clip_query[:, :, :, None] == clip_keys[:, :, None, :]) & banded)[:, :, None]


def attend_forward(query, key_pad, value_pad, clip_query, clip_keys, block_rows):
    seqs, rows_all, heads_here, head_width = query.shape
    span_keys = block_rows + WINDOW
    scaling = 1.0 / math.sqrt(head_width)
    count = block_rows // block_rows

    def one_block(index):
        start = index * block_rows
        query_blk = lax.dynamic_slice_in_dim(query, start, block_rows, 1).reshape(
            seqs, count, block_rows, heads_here, head_width
        )
        key_blk = key_tiles(lax.dynamic_slice_in_dim(key_pad, start, span_keys, 1))
        value_blk = key_tiles(lax.dynamic_slice_in_dim(value_pad, start, span_keys, 1))
        clip_q = lax.dynamic_slice_in_dim(clip_query, start, block_rows, 1).reshape(
            seqs, count, block_rows
        )
        clip_k = key_tiles(lax.dynamic_slice_in_dim(clip_keys, start, span_keys, 1))
        allowed = band_allowed(clip_q, clip_k, block_rows)
        scores = (
            jnp.einsum("snqhd,snkhd->snhqk", query_blk, key_blk, preferred_element_type=jnp.float32)
            * scaling
        )
        masked = jnp.where(allowed, scores, -1e30)
        row_max = jnp.max(masked, axis=-1, keepdims=True)
        exp_terms = jnp.where(allowed, jnp.exp(masked - row_max), 0.0)
        row_sum = jnp.sum(exp_terms, axis=-1, keepdims=True)
        attn_probs = (exp_terms / row_sum).astype(jnp.bfloat16)
        mixed_blk = jnp.einsum(
            "snhqk,snkhd->snqhd", attn_probs, value_blk, preferred_element_type=jnp.float32
        ).astype(jnp.bfloat16)
        mixed_blk = mixed_blk.reshape(seqs, block_rows, heads_here, head_width)
        lse = (
            (row_max[..., 0] + jnp.log(row_sum[..., 0]))
            .transpose(0, 2, 1, 3)
            .reshape(seqs, heads_here, block_rows)
        )
        return (mixed_blk, lse)

    mixed, log_totals = lax.map(one_block, jnp.arange(rows_all // block_rows, dtype=jnp.int32))
    mixed = jnp.moveaxis(mixed, 0, 1).reshape(seqs, rows_all, heads_here, head_width)
    log_totals = jnp.moveaxis(log_totals, 0, 2).reshape(seqs, heads_here, rows_all)
    return (mixed, log_totals)


def attend_backward(
    query, key_pad, value_pad, clip_query, clip_keys, log_totals, grad_mixed, block_rows
):
    seqs, rows_all, heads_here, head_width = query.shape
    span_keys = block_rows + WINDOW
    scaling = 1.0 / math.sqrt(head_width)
    count = block_rows // block_rows

    def one_block(carry, index):
        key_acc, value_acc = carry
        start = index * block_rows
        query_blk = lax.dynamic_slice_in_dim(query, start, block_rows, 1).reshape(
            seqs, count, block_rows, heads_here, head_width
        )
        key_blk = key_tiles(lax.dynamic_slice_in_dim(key_pad, start, span_keys, 1))
        value_blk = key_tiles(lax.dynamic_slice_in_dim(value_pad, start, span_keys, 1))
        clip_q = lax.dynamic_slice_in_dim(clip_query, start, block_rows, 1).reshape(
            seqs, count, block_rows
        )
        clip_k = key_tiles(lax.dynamic_slice_in_dim(clip_keys, start, span_keys, 1))
        allowed = band_allowed(clip_q, clip_k, block_rows)
        lse_blk = (
            lax.dynamic_slice_in_dim(log_totals, start, block_rows, 2)
            .reshape(seqs, heads_here, count, block_rows)
            .transpose(0, 2, 1, 3)
        )
        grad_blk = lax.dynamic_slice_in_dim(grad_mixed, start, block_rows, 1).reshape(
            seqs, count, block_rows, heads_here, head_width
        )
        scores = (
            jnp.einsum("snqhd,snkhd->snhqk", query_blk, key_blk, preferred_element_type=jnp.float32)
            * scaling
        )
        masked = jnp.where(allowed, scores, -1e30)
        attn_probs = jnp.where(allowed, jnp.exp(masked - lse_blk[..., None]), 0.0)
        grad_probs = jnp.einsum(
            "snqhd,snkhd->snhqk", grad_blk, value_blk, preferred_element_type=jnp.float32
        )
        delta = jnp.sum(attn_probs * grad_probs, axis=-1, keepdims=True)
        grad_scores = (attn_probs * (grad_probs - delta)).astype(jnp.bfloat16)
        grad_query = (
            jnp.einsum(
                "snhqk,snkhd->snqhd", grad_scores, key_blk, preferred_element_type=jnp.float32
            )
            * scaling
        )
        grad_key = (
            jnp.einsum(
                "snhqk,snqhd->snkhd", grad_scores, query_blk, preferred_element_type=jnp.float32
            )
            * scaling
        )
        grad_value = jnp.einsum(
            "snhqk,snqhd->snkhd",
            attn_probs.astype(jnp.bfloat16),
            grad_blk,
            preferred_element_type=jnp.float32,
        )
        grad_key = untile_keys(grad_key)
        grad_value = untile_keys(grad_value)
        key_acc = lax.dynamic_update_slice_in_dim(
            key_acc, lax.dynamic_slice_in_dim(key_acc, start, span_keys, 1) + grad_key, start, 1
        )
        value_acc = lax.dynamic_update_slice_in_dim(
            value_acc,
            lax.dynamic_slice_in_dim(value_acc, start, span_keys, 1) + grad_value,
            start,
            1,
        )
        return ((key_acc, value_acc), grad_query.reshape(seqs, block_rows, heads_here, head_width))

    zero_pad = jnp.zeros(key_pad.shape, jnp.float32)
    (key_grads, value_grads), query_grads = lax.scan(
        one_block, (zero_pad, zero_pad), jnp.arange(rows_all // block_rows, dtype=jnp.int32)
    )
    query_grads = jnp.moveaxis(query_grads, 0, 1).reshape(seqs, rows_all, heads_here, head_width)
    return (query_grads, key_grads, value_grads)


def rows_dot(left, right):
    return jnp.dot(left, right, preferred_element_type=jnp.float32)


def column_sum(left, right):
    return jnp.sum(left * right, axis=0)


def outer_rows(left, right):
    return jnp.einsum("rc,re->ce", left, right, preferred_element_type=jnp.float32)


def on_device(
    frames,
    clip_ids,
    norm_gain,
    w_query,
    w_key,
    w_value,
    w_output,
    attn_scale,
    mlp_gain,
    w_gate,
    w_up,
    w_down,
    mlp_scale,
    out_grad,
):
    seqs, local_len, width = frames.shape
    full_len = clip_ids.shape[1]
    rows_count = seqs * local_len
    half_span = WINDOW // 2
    heads_all = width // HEAD_DIM
    local_shape = (seqs, local_len, heads_all, HEAD_DIM)
    hidden_width = w_gate.shape[1]
    ratio = hidden_width // width
    own_rows = width // lax.axis_size(("seq", "sp"))
    inputs = frames.astype(jnp.float32).reshape(rows_count, width)
    centered = inputs - jnp.mean(inputs, axis=-1, keepdims=True)
    inv_ln = lax.rsqrt(jnp.mean(centered * centered, axis=-1, keepdims=True) + ln_eps)
    unit_ln = centered * inv_ln
    normed_low = (unit_ln * norm_gain).astype(jnp.bfloat16)
    cos_full, sin_full = rotary_tables(clip_positions(clip_ids))
    offset = lax.axis_index("sp") * local_len
    cos_here = lax.dynamic_slice_in_dim(cos_full, offset, local_len, 1)
    sin_here = lax.dynamic_slice_in_dim(sin_full, offset, local_len, 1)
    query_time = rotate(
        rows_dot(normed_low, w_query).reshape(local_shape), cos_here, sin_here
    ).astype(jnp.bfloat16)
    key_time = rotate(rows_dot(normed_low, w_key).reshape(local_shape), cos_here, sin_here).astype(
        jnp.bfloat16
    )
    value_time = rows_dot(normed_low, w_value).astype(jnp.bfloat16).reshape(local_shape)
    clip_pad = jnp.pad(clip_ids, ((0, 0), (half_span, half_span)), constant_values=-1)
    pad_spec = ((0, 0), (half_span, half_span), (0, 0), (0, 0))
    query_head, key_head, value_head = (
        lax.all_to_all(
            query_time.reshape(seqs, local_len, width),
            "sp",
            split_axis=2,
            concat_axis=1,
            tiled=True,
        ),
        lax.all_to_all(
            key_time.reshape(seqs, local_len, width), "sp", split_axis=2, concat_axis=1, tiled=True
        ),
        lax.all_to_all(
            value_time.reshape(seqs, local_len, width),
            "sp",
            split_axis=2,
            concat_axis=1,
            tiled=True,
        ),
    )
    heads_here = query_head.shape[2] // HEAD_DIM
    head_shape = (seqs, full_len, heads_here, HEAD_DIM)
    query_use = query_head.reshape(head_shape)
    key_use = jnp.pad(key_head.reshape(head_shape), pad_spec)
    value_use = jnp.pad(value_head.reshape(head_shape), pad_spec)
    block_rows = BLOCK
    mixed_use, log_totals = attend_forward(
        query_use, key_use, value_use, clip_ids, clip_pad, block_rows
    )
    mixed_time = lax.all_to_all(
        mixed_use.reshape(seqs, full_len, heads_here * HEAD_DIM),
        "sp",
        split_axis=1,
        concat_axis=2,
        tiled=True,
    )
    mixed_rows = mixed_time.reshape(rows_count, width)
    attn_out = rows_dot(mixed_rows, w_output)
    middle = inputs + attn_scale * attn_out
    inv_rms = lax.rsqrt(jnp.mean(middle * middle, axis=-1, keepdims=True) + rms_eps)
    unit_rms = middle * inv_rms
    mlp_in = (unit_rms * mlp_gain).astype(jnp.bfloat16)
    gate_pre = rows_dot(mlp_in, w_gate)
    up_pre = rows_dot(mlp_in, w_up)
    hidden = (jax.nn.silu(gate_pre) * up_pre).astype(jnp.bfloat16)
    down_out = rows_dot(hidden, w_down)
    layer_out = (middle + mlp_scale * down_out).astype(jnp.bfloat16).reshape(seqs, local_len, width)
    grad_result = out_grad.astype(jnp.float32).reshape(rows_count, width)
    grad_down_in = (mlp_scale * grad_result).astype(jnp.bfloat16)
    grad_hidden = jnp.einsum("rd,fd->rf", grad_down_in, w_down, preferred_element_type=jnp.float32)
    sigmoid_gate = jax.nn.sigmoid(gate_pre)
    grad_gate = (
        grad_hidden * up_pre * sigmoid_gate * (1.0 + gate_pre * (1.0 - sigmoid_gate))
    ).astype(jnp.bfloat16)
    grad_up = (grad_hidden * gate_pre * sigmoid_gate).astype(jnp.bfloat16)
    grad_mlp_in = jnp.einsum(
        "rf,df->rd", grad_gate, w_gate, preferred_element_type=jnp.float32
    ) + jnp.einsum("rf,df->rd", grad_up, w_up, preferred_element_type=jnp.float32)
    scaled_rms = grad_mlp_in * mlp_gain
    grad_middle = grad_result + inv_rms * (
        scaled_rms - unit_rms * jnp.mean(scaled_rms * unit_rms, axis=-1, keepdims=True)
    )
    grad_attn_in = (attn_scale * grad_middle).astype(jnp.bfloat16)
    grad_mixed = jnp.einsum(
        "re,de->rd", grad_attn_in, w_output, preferred_element_type=jnp.float32
    ).astype(jnp.bfloat16)
    grad_use = lax.all_to_all(
        grad_mixed.reshape(seqs, local_len, width), "sp", split_axis=2, concat_axis=1, tiled=True
    ).reshape(head_shape)
    query_grads, key_grads, value_grads = attend_backward(
        query_use, key_use, value_use, clip_ids, clip_pad, log_totals, grad_use, block_rows
    )
    key_own = key_grads[:, half_span : half_span + full_len]
    value_own = value_grads[:, half_span : half_span + full_len]
    cos_use, sin_use = (cos_full, sin_full)
    grad_query_low = rotate_back(query_grads, cos_use, sin_use).astype(jnp.bfloat16)
    grad_key_low = rotate_back(key_own, cos_use, sin_use).astype(jnp.bfloat16)
    grad_value_low = value_own.astype(jnp.bfloat16)
    query_back, key_back, value_back = (
        lax.all_to_all(
            grad_query_low.reshape(seqs, full_len, heads_here * HEAD_DIM),
            "sp",
            split_axis=1,
            concat_axis=2,
            tiled=True,
        ),
        lax.all_to_all(
            grad_key_low.reshape(seqs, full_len, heads_here * HEAD_DIM),
            "sp",
            split_axis=1,
            concat_axis=2,
            tiled=True,
        ),
        lax.all_to_all(
            grad_value_low.reshape(seqs, full_len, heads_here * HEAD_DIM),
            "sp",
            split_axis=1,
            concat_axis=2,
            tiled=True,
        ),
    )
    query_back = query_back.reshape(rows_count, width)
    key_back = key_back.reshape(rows_count, width)
    value_back = value_back.reshape(rows_count, width)
    grad_normed = jnp.einsum("re,de->rd", query_back, w_query, preferred_element_type=jnp.float32)
    grad_normed = grad_normed + jnp.einsum(
        "re,de->rd", key_back, w_key, preferred_element_type=jnp.float32
    )
    grad_normed = grad_normed + jnp.einsum(
        "re,de->rd", value_back, w_value, preferred_element_type=jnp.float32
    )
    scaled_ln = grad_normed * norm_gain
    grad_ln = inv_ln * (
        scaled_ln
        - jnp.mean(scaled_ln, axis=-1, keepdims=True)
        - unit_ln * jnp.mean(scaled_ln * unit_ln, axis=-1, keepdims=True)
    )
    frames_grad = (grad_middle + grad_ln).astype(jnp.bfloat16).reshape(seqs, local_len, width)
    attn_cols = 4 * width + 2
    gate_part = outer_rows(mlp_in, grad_gate)
    up_part = outer_rows(mlp_in, grad_up)
    down_part = outer_rows(hidden, grad_down_in).reshape(
        own_rows * lax.axis_size(("seq", "sp")), ratio * width
    )
    gain_part = column_sum(grad_mlp_in, unit_rms)
    scale_part = column_sum(grad_result, down_out)
    query_part = outer_rows(normed_low, query_back)
    key_part = outer_rows(normed_low, key_back)
    value_part = outer_rows(normed_low, value_back)
    output_part = outer_rows(mixed_rows, grad_attn_in)
    attn_gain_part = column_sum(grad_normed, unit_ln)
    attn_scale_part = column_sum(grad_middle, attn_out)
    summed = lax.psum_scatter(
        jnp.concatenate(
            [
                jnp.concatenate(
                    [
                        query_part,
                        key_part,
                        value_part,
                        output_part,
                        attn_gain_part[:, None],
                        attn_scale_part[:, None],
                    ],
                    axis=1,
                ),
                jnp.concatenate(
                    [gate_part, up_part, down_part, gain_part[:, None], scale_part[:, None]], axis=1
                ),
            ],
            axis=1,
        ),
        ("seq", "sp"),
        scatter_dimension=0,
        tiled=True,
    )
    attn_summed = summed[:, :attn_cols]
    tail = 4 * width
    norm_grad = attn_summed[:, tail]
    query_grad = attn_summed[:, :width]
    key_grad = attn_summed[:, width : 2 * width]
    value_grad = attn_summed[:, 2 * width : 3 * width]
    output_grad = attn_summed[:, 3 * width : tail]
    attn_scale_grad = attn_summed[:, tail + 1]
    mlp_summed = summed[:, attn_cols:]
    gate_g = mlp_summed[:, :hidden_width]
    up_g = mlp_summed[:, hidden_width : 2 * hidden_width]
    down_g = mlp_summed[:, 2 * hidden_width : 2 * hidden_width + ratio * width].reshape(
        own_rows * ratio, width
    )
    tail = 2 * hidden_width + ratio * width
    mlp_norm_grad = mlp_summed[:, tail]
    mlp_scale_grad = mlp_summed[:, tail + 1]
    return (
        layer_out,
        frames_grad,
        norm_grad,
        query_grad,
        key_grad,
        value_grad,
        output_grad,
        attn_scale_grad,
        mlp_norm_grad,
        gate_g,
        up_g,
        down_g,
        mlp_scale_grad,
    )


def solution(mesh):
    placed = (
        P("seq", "sp", None),
        P("seq", None),
        P(),
        P(),
        P(),
        P(),
        P(),
        P(),
        P(),
        P(),
        P(),
        P(),
        P(),
        P("seq", "sp", None),
    )
    return jax.shard_map(
        on_device,
        mesh=mesh,
        in_specs=placed,
        out_specs=(
            P("seq", "sp", None),
            P("seq", "sp", None),
            P(("seq", "sp")),
            P(("seq", "sp"), None),
            P(("seq", "sp"), None),
            P(("seq", "sp"), None),
            P(("seq", "sp"), None),
            P(("seq", "sp")),
            P(("seq", "sp")),
            P(("seq", "sp"), None),
            P(("seq", "sp"), None),
            P(("seq", "sp"), None),
            P(("seq", "sp")),
        ),
        check_vma=False,
    )
```

profile of v0, /device:TPU:0, one launch (start us, length us, event | category | flops | bytes accessed | tf_op | source)
XLA Modules:
  0.0 1887.0 jit_solution(533394029982441799)
XLA Ops:
  16.0 9.6 copy.118
  26.1 13.0 reduce.25
  54.3 6.4 convolution_bitcast_fusion.1
  64.8 6.5 convolution_bitcast_fusion
  82.3 13.0 reduce.26
  104.6 6.1 copy.187
  110.8 13.0 reduce.27
  141.7 5.5 copy.155
  147.2 8.3 copy.120
  169.1 5.5 copy.156
  174.6 8.3 copy.124
  201.9 8.3 copy.128
  221.6 91.0 %while.26 = (s32[]{:T(128)}, bf16[2,1,832,8,64]{2,4,3,1,0:T(8,128)(2,1)}, f32[2,1,8,832]{3,2,1,0:T(8,128)S(1)}, s32[2]{0:T(128)S(1)}, bf16[1,1792,8,64]{1,3,2,0:...) while((s32[]{:T(128)}, ...), condition=%wide.region_7.8_spmd, body=%wide.region_4.7_spmd.sunk | while | flops 1730446848 | bytes 85748984 | solution.py:109
  223.9 13.9 fusion.163
  237.8 14.3 fusion.164
  252.1 15.2 fusion.165
  269.2 13.9 fusion.163
  283.1 14.3 fusion.164
  297.5 15.2 fusion.165
  312.7 5.5 copy.158
  318.2 12.4 reshape.773
  330.6 38.3 %reduce.28 = bf16[1664,512]{1,0:T(8,128)(2,1)} reduce(bf16[1664,1,512]{2,1,0:T(2,128)(2,1)} %bitcast.331, bf16[]{:T(256)} %broadcast.404), dimensions={1}, to_apply=%bitcast.211.reduce_sub_computation | reduce | bytes 3407874
  379.3 19.8 %all-to-all-done.3 = bf16[2,2,212992]{2,1,0:T(2,128)(2,1)} async-done(((bf16[2,2,212992]{2,1,0:T(2,128)(2,1)}), bf16[2,2,212992]{2,1,0:T(2,128)(2,1)}, u32[]{:S(2)}, u32[]{:S(2)}) %all-to-all-start.3) | async-done | bytes 1703968 | tf_op jit(solution)/shard_map/all_to_all | solution.py:277
  413.9 10.2 fusion.106
  424.2 10.3 fusion.105
  434.5 25.9 %multiply_convert_fusion.1 = (bf16[832,4096]{1,0:T(8,128)(2,1)}, bf16[832,4096]{1,0:T(8,128)(2,1)}, bf16[832,4096]{1,0:T(8,128)(2,1)}) fusion(f32[832,4096]{1,0:T(8,128)} %fusion.105, f32[832,4096]{1,0:T(8,128)} %fusion.106, bf16[4096,1024]{1,0:T(8,128)(2,1)} %param.29, bf16[1,832,1024]{2,1,0:T(8,128)(2,1)} %param.31, f32[1024]{0:T(1024)S(1)} %copy-done.43), kind=kOutput, calls=%fused_computation.65 | convolution fusion | flops 7036403712 | bytes 57806848 | tf_op jit(solution)/shard_map/rd,fd->rf/dot_general | solution.py:297
  460.4 11.8 fusion.107
  472.2 14.3 multiply_reduce_fusion.1
  486.6 14.9 fusion.89
  501.4 13.4 fusion.70
  519.8 9.7 copy.133
  529.5 11.7 reduce.29
  548.1 14.9 fusion.111
  578.4 8.3 copy.135
  595.0 299.3 %while.27 = (s32[]{:T(128)}, f32[1,1792,8,64]{1,3,2,0:T(8,128)}, f32[1,1792,8,64]{1,3,2,0:T(8,128)}, f32[2,1,832,8,64]{2,0,4,3,1:T(2,128)}, s32[2]{0:T(128)S(1)}...) while((s32[]{:T(128)}, f32[1,1792,8,64]{1,3,2,0:T(8,128)}, ...), condition=%wide.region_12.13_spmd, body=%wide.region_10.12_spmd.sunk | while | flops 4160030208 | bytes 278707616 | solution.py:187
  597.5 14.1 fusion.174
  611.6 23.6 %multiply_reduce_fusion.7 = (f32[8,832]{1,0:T(8,128)S(1)}, f32[8,832,960]{2,1,0:T(8,128)}) fusion(f32[8,832,960]{2,1,0:T(8,128)} %fusion.174, f32[8,832]{1,0:T(8,128)S(1)} %dynamic-slice_bitcast_fusion.2, bf16[1,1792,8,64]{1,3,2,0:T(8,128)(2,1)} %get-tuple-element.444, s32[]{:T(128)S(6)} %select_n.100, ...), kind=kOutput, calls=%fused_computation.30.clone.1 | convolution fusion | flops 856221184 | bytes 55640072 | tf_op jit(solution)/shard_map/while/body/eval_jaxpr/snqhd,snkhd->snhqk/dot_general | solution.py:145
  635.1 22.8 %multiply_convert_fusion.9 = bf16[8,832,960]{2,1,0:T(8,128)(2,1)} fusion(f32[8,832,960]{2,1,0:T(8,128)} %get-tuple-element.358, f32[8,832,960]{2,1,0:T(8,128)} %fusion.174, f32[8,832]{1,0:T(8,128)S(1)} %get-tuple-element.359), kind=kLoop, calls=%fused_computation.29.clone.1 | loop fusion | flops 19169280 | bytes 63924224 | tf_op jit(solution)/shard_map/while/body/eval_jaxpr/convert_element_type | solution.py:154
  657.9 11.9 bitcast_add_fusion.5
  669.9 10.2 dynamic_update_slice.28
  680.1 9.5 multiply_bitcast_fusion.2
  689.7 7.8 bitcast_add_fusion.4
  700.6 10.2 dynamic_update_slice.27
  710.8 33.8 %dynamic_update_slice.29 = f32[2,1,832,8,64]{2,0,4,3,1:T(2,128)} dynamic-update-slice(f32[2,1,832,8,64]{2,0,4,3,1:T(2,128)} %get-tuple-element.422, f32[1,1,832,8,64]{2,0,4,3,1:T(1,128)} %copy.190, s32[]{:T(128)S(6)} %copy.209, s32[]{:T(128)} %constant.56.clone.1..sunk.1, s32[]{:T(128)} %constant.56.clone.1..sunk.1, s32[]{:T(128)} %constant.56.clone.1..sunk.1, s32[]{:T(128)} %constant.56.clone.1..sunk.1) | dynamic-update-slice | bytes 3407876 | tf_op jit(solution)/shard_map/while/body/jit(dynamic_update_index_in_dim)/dynamic_update_slice | solution.py:187
  746.7 14.1 fusion.174
  760.7 23.6 %multiply_reduce_fusion.7 = (f32[8,832]{1,0:T(8,128)S(1)}, f32[8,832,960]{2,1,0:T(8,128)}) fusion(f32[8,832,960]{2,1,0:T(8,128)} %fusion.174, f32[8,832]{1,0:T(8,128)S(1)} %dynamic-slice_bitcast_fusion.2, bf16[1,1792,8,64]{1,3,2,0:T(8,128)(2,1)} %get-tuple-element.444, s32[]{:T(128)S(6)} %select_n.100, ...), kind=kOutput, calls=%fused_computation.30.clone.1 | convolution fusion | flops 856221184 | bytes 55640072 | tf_op jit(solution)/shard_map/while/body/eval_jaxpr/snqhd,snkhd->snhqk/dot_general | solution.py:145
  784.3 22.8 %multiply_convert_fusion.9 = bf16[8,832,960]{2,1,0:T(8,128)(2,1)} fusion(f32[8,832,960]{2,1,0:T(8,128)} %get-tuple-element.358, f32[8,832,960]{2,1,0:T(8,128)} %fusion.174, f32[8,832]{1,0:T(8,128)S(1)} %get-tuple-element.359), kind=kLoop, calls=%fused_computation.29.clone.1 | loop fusion | flops 19169280 | bytes 63924224 | tf_op jit(solution)/shard_map/while/body/eval_jaxpr/convert_element_type | solution.py:154
  807.0 11.8 bitcast_add_fusion.5
  818.9 10.5 dynamic_update_slice.28
  829.4 9.5 multiply_bitcast_fusion.2
  838.9 7.7 bitcast_add_fusion.4
  849.8 10.5 dynamic_update_slice.27
  860.3 33.8 %dynamic_update_slice.29 = f32[2,1,832,8,64]{2,0,4,3,1:T(2,128)} dynamic-update-slice(f32[2,1,832,8,64]{2,0,4,3,1:T(2,128)} %get-tuple-element.422, f32[1,1,832,8,64]{2,0,4,3,1:T(1,128)} %copy.190, s32[]{:T(128)S(6)} %copy.209, s32[]{:T(128)} %constant.56.clone.1..sunk.1, s32[]{:T(128)} %constant.56.clone.1..sunk.1, s32[]{:T(128)} %constant.56.clone.1..sunk.1, s32[]{:T(128)} %constant.56.clone.1..sunk.1) | dynamic-update-slice | bytes 3407876 | tf_op jit(solution)/shard_map/while/body/jit(dynamic_update_index_in_dim)/dynamic_update_slice | solution.py:187
  904.9 6.3 copy.137
  911.2 37.1 %reduce.31 = bf16[1664,512]{1,0:T(8,128)(2,1)S(1)} reduce(bf16[1664,1,512]{2,1,0:T(2,128)(2,1)} %bitcast.329, bf16[]{:T(256)} %broadcast.404), dimensions={1}, to_apply=%bitcast.215.reduce_sub_computation | reduce | bytes 3407874
  954.3 14.9 fusion.110
  971.5 20.4 %reshape.765 = f32[1024,4096]{1,0:T(8,128)} reshape(f32[4096,1024]{1,0:T(8,128)} %fusion.89) | data formatting | bytes 33554432 | tf_op jit(solution)/shard_map/reshape | solution.py:369
  991.8 6.9 fusion.93
  1000.1 8.8 copy.139
  1008.9 38.7 %reduce.32 = bf16[1664,512]{1,0:T(8,128)(2,1)} reduce(bf16[1664,1,512]{2,1,0:T(2,128)(2,1)} %bitcast.330, bf16[]{:T(256)} %broadcast.404), dimensions={1}, to_apply=%bitcast.217.reduce_sub_computation | reduce | bytes 3407874
  1055.0 8.8 copy.141
  1063.9 38.3 %reduce.30 = bf16[1664,512]{1,0:T(8,128)(2,1)} reduce(bf16[1664,1,512]{2,1,0:T(2,128)(2,1)} %bitcast.328, bf16[]{:T(256)} %broadcast.404), dimensions={1}, to_apply=%bitcast.219.reduce_sub_computation | reduce | bytes 3407874
  1171.1 96.2 %concatenate.35 = f32[1024,16388]{1,0:T(8,128)} concatenate(f32[1024,1024]{1,0:T(8,128)} %fusion.76, f32[1024,1024]{1,0:T(8,128)} %fusion.80, f32[1024,1024]{1,0:T(8,128)} %fusion.78, f32[1024,1024]{1,0:T(8,128)} %fusion.93, f32[1024,1]{1,0:T(8,128)S(1)} %copy.147, f32[1024,1]{1,0:T(8,128)} %copy.148, f32[1024,4096]{1,0:T(8,128)} %fusion.110, f32[1024,4096]{1,0:T(8,128)} %fusion.111, ...), dimensions={1} | concatenate | bytes 134250496 | tf_op jit(solution)/shard_map/concatenate | solution.py:381
  1272.6 600.1 %reduce-scatter.2.cloned.1.call-done = f32[32,16388]{1,0:T(8,128)} async-done(((f32[1024,16388]{1,0:T(8,128)}), f32[32,16388]{1,0:T(8,128)}) %reduce-scatter.2.cloned.1.call-update) | async-done | bytes 2097680 | tf_op jit(solution)/shard_map/reduce_scatter | solution.py:380
  (262 shorter events, 290.8 us)
Async XLA Ops:
  7.2 400.5 %copy-start = (bf16[1024,1024]{1,0:T(8,128)(2,1)S(1)}, bf16[1024,1024]{1,0:T(8,128)(2,1)}, u32[]{:S(2)}) copy-start(bf16[1024,1024]{1,0:T(8,128)(2,1)} %param.24) | copy-start | bytes 6291460
  7.2 4.0 copy-start.7
  7.2 4.0 copy-start.34
  9.1 55.6 %copy-start.29 = (f32[832]{0:T(1024)}, f32[832]{0:T(1024)S(1)}, u32[]{:S(2)}) copy-start(f32[832]{0:T(1024)S(1)} %broadcast_multiply_fusion.4) | copy-start | bytes 9988
  11.2 53.5 %copy-start.31 = (f32[832]{0:T(1024)}, f32[832]{0:T(1024)S(1)}, u32[]{:S(2)}) copy-start(f32[832]{0:T(1024)S(1)} %add_rsqrt_fusion.1) | copy-start | bytes 9988
  39.1 9.2 copy-start.23
  43.3 56.7 %all-to-all-start = ((bf16[2,2,212992]{2,1,0:T(2,128)(2,1)}), bf16[2,2,212992]{2,1,0:T(2,128)(2,1)}, u32[]{:S(2)}, u32[]{:S(2)}) async-start(bf16[2,2,212992]{2,1,0:T(2,128)(2,1)} %reshape.784), calls=%async_computation | async-start | bytes 3407872 | tf_op jit(solution)/shard_map/all_to_all | solution.py:260
  48.3 22.9 %copy-start.39 = (f32[32]{0:T(128)}, f32[32]{0:T(128)S(1)}, u32[]{:S(2)}) copy-start(f32[32]{0:T(128)S(1)} %multiply_exponential_fusion) | copy-start | bytes 388
  50.4 20.9 %copy-start.27 = (f32[1664]{0:T(1024)}, f32[1664]{0:T(1024)S(1)}, u32[]{:S(2)}) copy-start(f32[1664]{0:T(1024)S(1)} %fusion.95) | copy-start | bytes 19972
  100.0 28.1 %all-to-all-start.1 = ((bf16[2,2,212992]{2,1,0:T(2,128)(2,1)}), bf16[2,2,212992]{2,1,0:T(2,128)(2,1)}, u32[]{:S(2)}, u32[]{:S(2)}) async-start(bf16[2,2,212992]{2,1,0:T(2,128)(2,1)} %reshape.786), calls=%async_computation.1 | async-start | bytes 3407872 | tf_op jit(solution)/shard_map/all_to_all | solution.py:250
  128.0 59.7 %all-to-all-start.2 = ((bf16[2,2,212992]{2,1,0:T(2,128)(2,1)}), bf16[2,2,212992]{2,1,0:T(2,128)(2,1)}, u32[]{:S(2)}, u32[]{:S(2)}) async-start(bf16[2,2,212992]{2,1,0:T(2,128)(2,1)} %reshape.788), calls=%async_computation.2 | async-start | bytes 3407872 | tf_op jit(solution)/shard_map/all_to_all | solution.py:257
  215.1 4.1 copy-start.10
  312.6 17.9 copy-start.25
  368.9 8.0 copy-start.28
  368.9 8.0 copy-start.40
  372.2 26.9 %all-to-all-start.3 = ((bf16[2,2,212992]{2,1,0:T(2,128)(2,1)}), bf16[2,2,212992]{2,1,0:T(2,128)(2,1)}, u32[]{:S(2)}, u32[]{:S(2)}) async-start(bf16[2,2,212992]{2,1,0:T(2,128)(2,1)} %reshape.790), calls=%async_computation.3 | async-start | bytes 3407872 | tf_op jit(solution)/shard_map/all_to_all | solution.py:277
  405.4 2.3 copy-start.8
  407.7 4.0 copy-start.19
  407.7 6.2 slice-start.2
  407.7 5.8 copy-start.33
  407.8 6.1 slice-start.3
  413.5 10.6 slice-start
  413.9 10.3 copy-start.18
  413.9 10.3 slice-start.1
  424.2 10.3 copy-start.43
  460.4 11.8 copy-start.12
  460.4 41.1 %slice-start.4 = ((s8[8388608]{0:T(1024)(128)(4,1)}), s8[4194304]{0:T(1024)(128)(4,1)S(1)}, s32[]{:S(2)}) async-start(s8[8388608]{0:T(1024)(128)(4,1)} %bitcast.377), calls=%async_computation.14 | async-start | bytes 8388608
  472.2 14.4 copy-start.42
  472.2 29.2 %slice-start.5 = ((s8[8388608]{0:T(1024)(128)(4,1)}), s8[4194304]{0:T(1024)(128)(4,1)S(1)}, s32[]{:S(2)}) async-start(s8[8388608]{0:T(1024)(128)(4,1)} %bitcast.377), calls=%async_computation.15 | async-start | bytes 8388608
  501.4 15.2 copy-start.45
  544.4 24.0 %all-to-all-start.4 = ((bf16[2,2,212992]{2,1,0:T(2,128)(2,1)}), bf16[2,2,212992]{2,1,0:T(2,128)(2,1)S(1)}, u32[]{:S(2)}, u32[]{:S(2)}) async-start(bf16[2,2,212992]{2,1,0:T(2,128)(2,1)} %reshape.792), calls=%async_computation.4 | async-start | bytes 3407872 | tf_op jit(solution)/shard_map/all_to_all | solution.py:314
  590.7 4.2 copy-start.22
  590.8 4.2 copy-start.24
  590.8 4.2 copy-start.26
  595.4 16.1 copy-start.4
  635.1 22.8 %copy-start.6 = (f32[1,1792,8,64]{1,3,2,0:T(8,128)S(1)}, f32[1,1792,8,64]{1,3,2,0:T(8,128)}, u32[]{:S(2)}) copy-start(f32[1,1792,8,64]{1,3,2,0:T(8,128)} %get-tuple-element.421) | copy-start | bytes 11010052 | tf_op jit(solution)/shard_map/while
  680.1 9.6 copy-start.2
  680.1 9.6 copy-start.3
  710.8 33.8 %copy-start.5 = (bf16[1,1664,8,64]{1,3,2,0:T(8,128)(2,1)S(1)}, bf16[1,1664,8,64]{1,3,2,0:T(8,128)(2,1)}, u32[]{:S(2)}) copy-start(bf16[1,1664,8,64]{1,3,2,0:T(8,128)(2,1)} %copy-done.4) | copy-start | bytes 5111812 | tf_op jit(solution)/shard_map/while
  744.6 16.1 copy-start.4
  784.3 22.8 %copy-start.6 = (f32[1,1792,8,64]{1,3,2,0:T(8,128)S(1)}, f32[1,1792,8,64]{1,3,2,0:T(8,128)}, u32[]{:S(2)}) copy-start(f32[1,1792,8,64]{1,3,2,0:T(8,128)} %get-tuple-element.421) | copy-start | bytes 11010052 | tf_op jit(solution)/shard_map/while
  829.4 9.5 copy-start.2
  829.4 9.5 copy-start.3
  860.3 33.8 %copy-start.5 = (bf16[1,1664,8,64]{1,3,2,0:T(8,128)(2,1)S(1)}, bf16[1,1664,8,64]{1,3,2,0:T(8,128)(2,1)}, u32[]{:S(2)}) copy-start(bf16[1,1664,8,64]{1,3,2,0:T(8,128)(2,1)} %copy-done.4) | copy-start | bytes 5111812 | tf_op jit(solution)/shard_map/while
  894.3 5.5 copy-start.20
  894.3 5.5 copy-start.21
  950.5 155.1 %all-to-all-start.5 = ((bf16[2,2,212992]{2,1,0:T(2,128)(2,1)}), bf16[2,2,212992]{2,1,0:T(2,128)(2,1)S(1)}, u32[]{:S(2)}, u32[]{:S(2)}) async-start(bf16[2,2,212992]{2,1,0:T(2,128)(2,1)} %reshape.794), calls=%async_computation.5 | async-start | bytes 3407872 | tf_op jit(solution)/shard_map/all_to_all | solution.py:327
  954.2 14.9 copy-start.38
  954.2 15.1 copy-start.36
  954.3 16.2 copy-start.37
  971.5 20.4 %copy-start.46 = (f32[1024]{0:T(1024)S(1)}, f32[1024]{0:T(1024)}, u32[]{:S(2)}) copy-start(f32[1024]{0:T(1024)} %param.25) | copy-start | bytes 12292
  991.8 6.9 copy-start.14
  1105.7 24.2 %all-to-all-start.6 = ((bf16[2,2,212992]{2,1,0:T(2,128)(2,1)}), bf16[2,2,212992]{2,1,0:T(2,128)(2,1)}, u32[]{:S(2)}, u32[]{:S(2)}) async-start(bf16[2,2,212992]{2,1,0:T(2,128)(2,1)} %reshape.796), calls=%async_computation.6 | async-start | bytes 3407872 | tf_op jit(solution)/shard_map/all_to_all | solution.py:334
  1117.7 3.7 copy-start.9
  1117.7 3.7 copy-start.30
  1117.7 3.7 copy-start.32
  1117.7 3.7 copy-start.35
  1129.8 23.3 %all-to-all-start.7 = ((bf16[2,2,212992]{2,1,0:T(2,128)(2,1)}), bf16[2,2,212992]{2,1,0:T(2,128)(2,1)}, u32[]{:S(2)}, u32[]{:S(2)}) async-start(bf16[2,2,212992]{2,1,0:T(2,128)(2,1)} %reshape.798), calls=%async_computation.7 | async-start | bytes 3407872 | tf_op jit(solution)/shard_map/all_to_all | solution.py:341
  1134.5 738.2 %reduce-scatter.2.cloned.1.call-start = ((), (), s32[]{:S(2)}) async-start(), calls=%async_computation.9 | async-start | bytes 69746688 | tf_op jit(solution)/shard_map/reduce_scatter | solution.py:380
  1161.8 4.7 copy-start.41
  1161.8 4.7 copy-start.47
  1161.8 4.7 copy-start.48
  1166.5 4.7 copy-start.15
  1267.4 612.5 %copy-start.1 = (bf16[1024,1024]{1,0:T(8,128)(2,1)S(1)}, bf16[1024,1024]{1,0:T(8,128)(2,1)}, u32[]{:S(2)}) copy-start(bf16[1024,1024]{1,0:T(8,128)(2,1)} %param.24) | copy-start | bytes 6291460
  (5 other events, 10.3 us)
Sparse Core Ops, SparseCore 0:
  1267.5 605.1 reduce-scatter.1
where the time goes:
time: 1910 us; the launch traced here: 1890 us
  waiting for transfers between devices  631 us (33%)
  local copies, waits for them, and re-layouts  518 us (27%)
  matrix products  380 us (20%)
  other arithmetic  303 us (16%)
  starting transfers between devices  35.7 us (2%)
    reduce_scatter x1, waiting for transfers between devices, on_device(): lax.psum_scatter(jnp.concatenate([jnp.concatenate([query_part, key_part,...  600 us
    unnamed x11, other arithmetic  203 us
    unnamed x131, local copies, waits for them, and re-layouts  99.8 us
    concatenate x1, local copies, waits for them, and re-layouts, on_device(): jnp.concatenate([jnp.concatenate([query_part, key_part, value_part, outpu...  96.2 us
    dot_general x4, matrix products, one_block(): jnp.einsum('snqhd,snkhd->snhqk', query_blk, key_blk, preferred_element_ty...  75 us
    dynamic_update_slice x4, local copies, waits for them, and re-layouts, attend_backward(): lax.scan(one_block, (zero_pad, zero_pad), jnp.arange(rows_all // block_ro...  73.9 us
    dot_general x7, matrix products, outer_rows(): jnp.einsum('rc,re->ce', left, right, preferred_element_type=jnp.float32)  65.5 us
    dot_general x7, matrix products, rows_dot(): return jnp.dot(left, right, preferred_element_type=jnp.float32)  55.5 us
  transfers between devices with their start and end apart: 9, of which 5 were waited for; matrix products, arithmetic and copies ran while one was open for 18% of the time, Pallas kernels for 0%

commit v1 on v0

v1 whole, which is shorter than its diff:
```python
import functools
import math

import jax
import jax.numpy as jnp
import numpy as np
from jax import lax
from jax.experimental import pallas as pl
from jax.experimental.pallas import tpu as pltpu
from jax.sharding import PartitionSpec as P

HEAD_DIM = 64
HALF = 64
LANES = 128
GROUP = 256
GH = GROUP // HEAD_DIM
QB = 128
KB = QB + 2 * HALF
LN_EPS = 1e-05
RMS_EPS = 1e-06
VMEM = 58 << 20
F32 = jnp.float32
BF16 = jnp.bfloat16

NT = (((1,), (1,)), ((), ()))
NN = (((1,), (0,)), ((), ()))
TN = (((0,), (0,)), ((), ()))


def dot(a, b, dims=NN):
    return lax.dot_general(a, b, dims, preferred_element_type=F32)


def params(grid=0):
    kinds = ("arbitrary",) * grid if grid else None
    return pltpu.CompilerParams(vmem_limit_bytes=VMEM, dimension_semantics=kinds)


def cost(flops, moved, trans=0):
    return pl.CostEstimate(
        flops=int(flops), bytes_accessed=int(moved), transcendentals=int(trans)
    )


def whole(shape):
    return pl.BlockSpec(shape, lambda *_: (0,) * len(shape))


def swap_halves(v):
    lane = lax.broadcasted_iota(jnp.int32, v.shape, 1)
    return jnp.where(lane % HEAD_DIM < HEAD_DIM // 2, pltpu.roll(v, 96, 1), pltpu.roll(v, 32, 1))


def rotated(v, cos_tab, sin_tab, sign):
    pieces = []
    for at in range(0, v.shape[1], LANES):
        part = v[:, at : at + LANES]
        turned = swap_halves(part) * sin_tab
        pieces.append(part * cos_tab + turned if sign > 0 else part * cos_tab - turned)
    return jnp.concatenate(pieces, axis=1)


def project_kernel(with_query, x_ref, gain_ref, cos_ref, sin_ref, *refs):
    count = 3 if with_query else 2
    weights, outs = refs[:count], refs[count:]
    normed_ref, outs = outs[0], outs[1:]
    step = pl.program_id(0)
    blocks = weights[0].shape[0] // GROUP

    @pl.when(step == 0)
    def _():
        x = x_ref[...].astype(F32)
        centered = x - jnp.mean(x, axis=-1, keepdims=True)
        inv = lax.rsqrt(jnp.mean(centered * centered, axis=-1, keepdims=True) + LN_EPS)
        normed_ref[...] = (centered * inv * gain_ref[...]).astype(BF16)

    for which in range(count):

        @pl.when(step // blocks == which)
        def _(which=which):
            out = dot(normed_ref[...], weights[which][...])
            if which < count - 1:
                out = rotated(out, cos_ref[...], sin_ref[...], 1)
            if with_query and which == 0:
                out = out * (1.0 / math.sqrt(HEAD_DIM))
            outs[which][...] = out.astype(BF16)


def project(x, gain, cos_tab, sin_tab, weights):
    rows, width = x.shape
    with_query = len(weights) == 3
    blocks = width // GROUP
    grid = blocks * len(weights)

    def at(which):
        return lambda j: (0, jnp.clip(j - which * blocks, 0, blocks - 1))

    out = jax.ShapeDtypeStruct((rows, width), BF16)
    return pl.pallas_call(
        functools.partial(project_kernel, with_query),
        grid=(grid,),
        in_specs=[
            whole((rows, width)),
            whole((1, width)),
            whole((rows, LANES)),
            whole((rows, LANES)),
        ]
        + [pl.BlockSpec((width, GROUP), at(w)) for w in range(len(weights))],
        out_specs=[whole((rows, width))]
        + [pl.BlockSpec((rows, GROUP), at(w)) for w in range(len(weights))],
        out_shape=[out] * (1 + len(weights)),
        compiler_params=params(1),
        cost_estimate=cost(
            2 * rows * width * width * len(weights),
            2 * len(weights) * width * width + 2 * rows * width * (2 + len(weights)),
        ),
        name="project_rows" if with_query else "project_halo",
    )(x, gain, cos_tab, sin_tab, *weights)


def stack_heads(block):
    lane = lax.broadcasted_iota(jnp.int32, block.shape, 1)
    zero = jnp.zeros_like(block)
    return jnp.concatenate(
        [jnp.where(lane // HEAD_DIM == h, block, zero) for h in range(GH)], axis=0
    )


def fill_keys(buf, own_ref, halo_ref, length):
    buf[0:HALF, :] = halo_ref[0:HALF, :]
    buf[HALF : HALF + length, :] = own_ref[...]
    buf[HALF + length : 2 * HALF + length, :] = halo_ref[HALF : 2 * HALF, :]
    rest = buf.shape[0] - 2 * HALF - length
    if rest:
        buf[2 * HALF + length :, :] = jnp.zeros((rest, buf.shape[1]), buf.dtype)


def fill_queries(buf, own_ref, length):
    buf[0:length, :] = own_ref[...]
    rest = buf.shape[0] - length
    if rest:
        buf[length:, :] = jnp.zeros((rest, buf.shape[1]), buf.dtype)


def attend_kernel(span_ref, q_ref, k_ref, v_ref, kh_ref, vh_ref, o_ref, p_ref, kbuf, vbuf, qbuf, vt, ot):
    length = q_ref.shape[0]
    padded = qbuf.shape[0]
    fill_keys(kbuf, k_ref, kh_ref, length)
    fill_keys(vbuf, v_ref, vh_ref, length)
    fill_queries(qbuf, q_ref, length)
    vt[...] = vbuf[...].T
    for b in range(padded // QB):
        q4 = stack_heads(qbuf[b * QB : (b + 1) * QB, :])
        scores = dot(kbuf[b * QB : b * QB + KB, :], q4, NT)
        place = lax.broadcasted_iota(jnp.int32, (KB, QB), 0) + b * QB
        low = span_ref[0, 0:1, b * QB : (b + 1) * QB]
        high = span_ref[0, 1:2, b * QB : (b + 1) * QB]
        seen = (place >= low) & (place < high)
        for h in range(GH):
            masked = jnp.where(seen, scores[:, h * QB : (h + 1) * QB], -1e30)
            terms = jnp.exp(masked - jnp.max(masked, axis=0, keepdims=True))
            total = jnp.sum(terms, axis=0, keepdims=True)
            probs = (terms * (1.0 / total)).astype(BF16)
            p_ref[:, b * GH * QB + h * QB : b * GH * QB + (h + 1) * QB] = probs
            ot[h * HEAD_DIM : (h + 1) * HEAD_DIM, b * QB : (b + 1) * QB] = dot(
                vt[h * HEAD_DIM : (h + 1) * HEAD_DIM, b * QB : b * QB + KB], probs
            ).astype(BF16)
    o_ref[...] = ot[...].T[0:length, :]


def attend(span, query, key, value, key_halo, value_halo, seqs):
    rows, width = query.shape
    length = rows // seqs
    padded = span.shape[2]
    groups = width // GROUP
    keys = padded + 2 * HALF
    own = pl.BlockSpec((length, GROUP), lambda s, g: (s, g))
    edge = pl.BlockSpec((2 * HALF, GROUP), lambda s, g: (s, g))
    return pl.pallas_call(
        attend_kernel,
        grid=(seqs, groups),
        in_specs=[
            pl.BlockSpec((1, 2, padded), lambda s, g: (s, 0, 0)),
            own,
            own,
            own,
            edge,
            edge,
        ],
        out_specs=[
            own,
            pl.BlockSpec((KB, GH * padded), lambda s, g: (s, g)),
        ],
        out_shape=[
            jax.ShapeDtypeStruct((rows, width), BF16),
            jax.ShapeDtypeStruct((seqs * KB, groups * GH * padded), BF16),
        ],
        scratch_shapes=[
            pltpu.VMEM((keys, GROUP), BF16),
            pltpu.VMEM((keys, GROUP), BF16),
            pltpu.VMEM((padded, GROUP), BF16),
            pltpu.VMEM((GROUP, keys), BF16),
            pltpu.VMEM((GROUP, padded), BF16),
        ],
        compiler_params=params(2),
        cost_estimate=cost(
            2 * 2 * seqs * width * padded * KB * 4, 2 * width * (4 * rows + KB * seqs * padded // 64)
        ),
        name="attend",
    )(span, query, key, value, key_halo, value_halo)


def attend_back_kernel(
    p_ref, q_ref, k_ref, v_ref, kh_ref, vh_ref, g_ref, cos_ref, sin_ref,
    dq_ref, dk_ref, dv_ref, dkh_ref, dvh_ref,
    kbuf, vbuf, qbuf, gbuf, kt, dqt, dkb, dvb,
):
    length = q_ref.shape[0]
    padded = qbuf.shape[0]
    fill_keys(kbuf, k_ref, kh_ref, length)
    fill_keys(vbuf, v_ref, vh_ref, length)
    fill_queries(qbuf, q_ref, length)
    fill_queries(gbuf, g_ref, length)
    kt[...] = kbuf[...].T
    dkb[...] = jnp.zeros_like(dkb)
    dvb[...] = jnp.zeros_like(dvb)
    for b in range(padded // QB):
        at, keys = slice(b * QB, (b + 1) * QB), slice(b * QB, b * QB + KB)
        q4 = stack_heads(qbuf[at, :])
        g4 = stack_heads(gbuf[at, :])
        probs = p_ref[:, b * GH * QB : (b + 1) * GH * QB]
        grads = dot(vbuf[keys, :], g4, NT)
        pieces = []
        for h in range(GH):
            part = probs[:, h * QB : (h + 1) * QB].astype(F32)
            grad = grads[:, h * QB : (h + 1) * QB]
            delta = jnp.sum(part * grad, axis=0, keepdims=True)
            low = (part * (grad - delta)).astype(BF16)
            pieces.append(low)
            dqt[h * HEAD_DIM : (h + 1) * HEAD_DIM, at] = dot(
                kt[h * HEAD_DIM : (h + 1) * HEAD_DIM, keys], low
            )
        dvb[keys, :] += dot(probs, g4)
        dkb[keys, :] += dot(jnp.concatenate(pieces, axis=1), q4)
    cos_tab, sin_tab = cos_ref[0], sin_ref[0]
    middle = slice(HALF, HALF + length)
    dq = dqt[...].T[0:length, :] * (1.0 / math.sqrt(HEAD_DIM))
    dq_ref[...] = rotated(dq, cos_tab[middle], sin_tab[middle], -1).astype(BF16)
    span = length + 2 * HALF
    dk = rotated(dkb[0:span, :], cos_tab, sin_tab, -1).astype(BF16)
    dk_ref[...] = dk[middle]
    dkh_ref[0:HALF, :] = dk[0:HALF]
    dkh_ref[HALF:, :] = dk[span - HALF :]
    dv_ref[...] = dvb[middle, :].astype(BF16)
    dvh_ref[0:HALF, :] = dvb[0:HALF, :].astype(BF16)
    dvh_ref[HALF:, :] = dvb[span - HALF : span, :].astype(BF16)


def attend_back(probs, query, key, value, key_halo, value_halo, grad, cos_tab, sin_tab, seqs):
    rows, width = query.shape
    length = rows // seqs
    padded = -(-length // QB) * QB
    groups = width // GROUP
    keys = padded + 2 * HALF
    own = pl.BlockSpec((length, GROUP), lambda s, g: (s, g))
    edge = pl.BlockSpec((2 * HALF, GROUP), lambda s, g: (s, g))
    table = pl.BlockSpec((1, length + 2 * HALF, LANES), lambda s, g: (s, 0, 0))
    out = jax.ShapeDtypeStruct((rows, width), BF16)
    out_edge = jax.ShapeDtypeStruct((seqs * 2 * HALF, width), BF16)
    return pl.pallas_call(
        attend_back_kernel,
        grid=(seqs, groups),
        in_specs=[
            pl.BlockSpec((KB, GH * padded), lambda s, g: (s, g)),
            own,
            own,
            own,
            edge,
            edge,
            own,
            table,
            table,
        ],
        out_specs=[own, own, own, edge, edge],
        out_shape=[out, out, out, out_edge, out_edge],
        scratch_shapes=[
            pltpu.VMEM((keys, GROUP), BF16),
            pltpu.VMEM((keys, GROUP), BF16),
            pltpu.VMEM((padded, GROUP), BF16),
            pltpu.VMEM((padded, GROUP), BF16),
            pltpu.VMEM((GROUP, keys), BF16),
            pltpu.VMEM((GROUP, padded), F32),
            pltpu.VMEM((keys, GROUP), F32),
            pltpu.VMEM((keys, GROUP), F32),
        ],
        compiler_params=params(2),
        cost_estimate=cost(
            2 * 4 * seqs * width * padded * KB * 4, 2 * width * (8 * rows + KB * seqs * padded // 64)
        ),
        name="attend_back",
    )(probs, query, key, value, key_halo, value_halo, grad, cos_tab, sin_tab)


def out_proj_kernel(m_ref, x_ref, w_ref, scale_ref, gain_ref, attn_ref, in_ref):
    attn = dot(m_ref[...], w_ref[...])
    attn_ref[...] = attn
    middle = x_ref[...].astype(F32) + scale_ref[...] * attn
    inv = lax.rsqrt(jnp.mean(middle * middle, axis=-1, keepdims=True) + RMS_EPS)
    in_ref[...] = (middle * inv * gain_ref[...]).astype(BF16)


def out_proj(mixed, x, w_output, scale, gain):
    rows, width = x.shape
    block = rows // 4
    row = pl.BlockSpec((block, width), lambda i: (i, 0))
    return pl.pallas_call(
        out_proj_kernel,
        grid=(rows // block,),
        in_specs=[row, row, whole((width, width)), whole((1, width)), whole((1, width))],
        out_specs=[row, row],
        out_shape=[
            jax.ShapeDtypeStruct((rows, width), F32),
            jax.ShapeDtypeStruct((rows, width), BF16),
        ],
        compiler_params=params(1),
        cost_estimate=cost(2 * rows * width * width, 2 * rows * width * 5 + 2 * width * width),
        name="out_proj",
    )(mixed, x, w_output, scale, gain)


def hidden_grad_kernel(core_ref, own_ref, peer_ref, scale_ref, w_ref, low_ref, out_ref):
    rows = own_ref.shape[0]

    @pl.when(pl.program_id(0) == 0)
    def _():
        low_ref[0:rows, :] = (own_ref[...].astype(F32) * scale_ref[...]).astype(BF16)
        low_ref[rows:, :] = (peer_ref[...].astype(F32) * scale_ref[...]).astype(BF16)

    for at in (0, rows):
        out_ref[at : at + rows, :] = dot(low_ref[at : at + rows, :], w_ref[...], NT).astype(BF16)


def hidden_grad(core, own, peer, scale, w_down, block):
    rows, width = own.shape
    count = w_down.shape[0] // block // 2
    return pl.pallas_call(
        hidden_grad_kernel,
        grid_spec=pltpu.PrefetchScalarGridSpec(
            num_scalar_prefetch=1,
            grid=(count,),
            in_specs=[
                whole((rows, width)),
                whole((rows, width)),
                whole((1, width)),
                pl.BlockSpec((block, width), lambda j, c: (2 * j + c[0], 0)),
            ],
            out_specs=[
                whole((2 * rows, width)),
                pl.BlockSpec((2 * rows, block), lambda j, c: (0, j)),
            ],
        ),
        out_shape=[
            jax.ShapeDtypeStruct((2 * rows, width), BF16),
            jax.ShapeDtypeStruct((2 * rows, count * block), BF16),
        ],
        compiler_params=params(1),
        cost_estimate=cost(
            4 * rows * width * count * block, 2 * (4 * rows * width + count * block * (width + 2 * rows))
        ),
        name="hidden_grad",
    )(core, own, peer, scale, w_down)


def feed_kernel(core_ref, xo_ref, xp_ref, gh_ref, wg_ref, wu_ref, *refs):
    hid_ref, gg_ref, gu_ref, gate_ref, up_ref, x_all = refs[-6:]
    rows = xo_ref.shape[0]

    @pl.when(pl.program_id(0) == 0)
    def _():
        x_all[0:rows, :] = xo_ref[...]
        x_all[rows:, :] = xp_ref[...]

    for at in (0, rows):
        part = slice(at, at + rows)
        gate = dot(x_all[part, :], wg_ref[...])
        up = dot(x_all[part, :], wu_ref[...])
        grad = gh_ref[part, :].astype(F32)
        sig = 1.0 / (1.0 + jnp.exp(-gate))
        act = gate * sig
        hid_ref[part, :] = (act * up).astype(BF16)
        gg_ref[part, :] = (grad * up * sig * (1.0 + gate * (1.0 - sig))).astype(BF16)
        gu_ref[part, :] = (grad * act).astype(BF16)
    gate_ref[...] = dot(x_all[...], gg_ref[...], TN).astype(BF16)
    up_ref[...] = dot(x_all[...], gu_ref[...], TN).astype(BF16)


def feed(core, x_own, x_peer, grad_hidden, w_gate, w_up, block, first, count, before):
    rows, width = x_own.shape
    half = grad_hidden.shape[1]
    wide = pl.BlockSpec((2 * rows, block), lambda j, c: (0, j + first))
    weight = pl.BlockSpec((width, block), lambda j, c: (0, 2 * (j + first) + c[0]))
    kept = jax.ShapeDtypeStruct((2 * rows, half), BF16)
    grads = jax.ShapeDtypeStruct((width, count * block), BF16)
    any_spec = pl.BlockSpec(memory_space=pl.ANY)
    return pl.pallas_call(
        feed_kernel,
        grid_spec=pltpu.PrefetchScalarGridSpec(
            num_scalar_prefetch=1,
            grid=(count,),
            in_specs=[whole((rows, width)), whole((rows, width)), wide, weight, weight]
            + [any_spec] * len(before),
            out_specs=[wide] * 3 + [pl.BlockSpec((width, block), lambda j, c: (0, j))] * 2,
            scratch_shapes=[pltpu.VMEM((2 * rows, width), BF16)],
        ),
        out_shape=[kept] * 3 + [grads] * 2,
        input_output_aliases={6 + i: i for i in range(len(before))},
        compiler_params=params(1),
        cost_estimate=cost(
            2 * 2 * rows * width * block * count * 4,
            2 * (4 * rows * width + count * block * (8 * rows + 4 * width)),
        ),
        name="feed",
    )(core, x_own, x_peer, grad_hidden, w_gate, w_up, *before)


def down_kernel(hid_ref, low_ref, one_ref, two_ref):
    out = dot(hid_ref[...], low_ref[...], TN).astype(BF16)
    half = one_ref.shape[1]
    one_ref[...] = out[:, :half]
    two_ref[...] = out[:, half:]


def down(hidden, low):
    rows, half = hidden.shape
    width = low.shape[1]
    block = 512
    return pl.pallas_call(
        down_kernel,
        grid=(half // block,),
        in_specs=[pl.BlockSpec((rows, block), lambda j: (0, j)), whole((rows, width))],
        out_specs=[pl.BlockSpec((block, width // 2), lambda j: (j, 0))] * 2,
        out_shape=[jax.ShapeDtypeStruct((half, width // 2), BF16)] * 2,
        compiler_params=params(1),
        cost_estimate=cost(
            2 * rows * half * width, 2 * (rows * half + rows * width + half * width)
        ),
        name="down_weight",
    )(hidden, low)


def feed_back_kernel(core_ref, *refs):
    pairs, (out_ref, acc) = len(refs[:-2]) // 3, refs[-2:]
    step = pl.program_id(0)
    block = refs[pairs].shape[1]
    total = None
    for i in range(pairs):
        for half, weight in enumerate(refs[pairs + 2 * i : pairs + 2 * i + 2]):
            part = dot(refs[i][:, half * block : (half + 1) * block], weight[...], NT)
            total = part if total is None else total + part

    @pl.when(step == 0)
    def _():
        acc[...] = total

    @pl.when((step > 0) & (step < pl.num_programs(0) - 1))
    def _():
        acc[...] += total

    @pl.when(step == pl.num_programs(0) - 1)
    def _():
        out_ref[...] = (acc[...] + total).astype(out_ref.dtype)


def feed_back(core, grads, weights, block, part, dtype):
    rows, half = grads[0].shape
    rows = rows // 2
    width = weights[0].shape[0]
    tall = pl.BlockSpec((rows, 2 * block), lambda j, c: (part, j))
    one = pl.BlockSpec((width, block), lambda j, c: (0, 4 * j + c[0]))
    two = pl.BlockSpec((width, block), lambda j, c: (0, 4 * j + 2 + c[0]))
    return pl.pallas_call(
        feed_back_kernel,
        grid_spec=pltpu.PrefetchScalarGridSpec(
            num_scalar_prefetch=1,
            grid=(half // block // 2,),
            in_specs=[tall] * len(grads) + [one, two] * len(weights),
            out_specs=whole((rows, width)),
            scratch_shapes=[pltpu.VMEM((rows, width), F32)],
        ),
        out_shape=jax.ShapeDtypeStruct((rows, width), dtype),
        compiler_params=params(1),
        cost_estimate=cost(
            2 * len(grads) * rows * half * width, 2 * len(grads) * (rows * half + half * width)
        ),
        name="feed_back",
    )(core, *grads, *[w for weight in weights for w in (weight, weight)])


def feed_out_kernel(core_ref, hid_ref, one_ref, two_ref, out_ref, acc):
    step = pl.program_id(0)
    block = one_ref.shape[0]
    total = dot(hid_ref[:, :block], one_ref[...]) + dot(hid_ref[:, block:], two_ref[...])

    @pl.when(step == 0)
    def _():
        acc[...] = total

    @pl.when((step > 0) & (step < pl.num_programs(0) - 1))
    def _():
        acc[...] += total

    @pl.when(step == pl.num_programs(0) - 1)
    def _():
        out_ref[...] = (acc[...] + total).astype(out_ref.dtype)


def feed_out(core, hidden, w_down, block, part, dtype):
    rows, half = hidden.shape
    rows = rows // 2
    width = w_down.shape[1]
    return pl.pallas_call(
        feed_out_kernel,
        grid_spec=pltpu.PrefetchScalarGridSpec(
            num_scalar_prefetch=1,
            grid=(half // block // 2,),
            in_specs=[
                pl.BlockSpec((rows, 2 * block), lambda j, c: (part, j)),
                pl.BlockSpec((block, width), lambda j, c: (4 * j + c[0], 0)),
                pl.BlockSpec((block, width), lambda j, c: (4 * j + 2 + c[0], 0)),
            ],
            out_specs=whole((rows, width)),
            scratch_shapes=[pltpu.VMEM((rows, width), F32)],
        ),
        out_shape=jax.ShapeDtypeStruct((rows, width), dtype),
        compiler_params=params(1),
        cost_estimate=cost(2 * rows * half * width, 2 * (rows * half + half * width)),
        name="feed_out",
    )(core, hidden, w_down, w_down)


def join_kernel(
    x_ref, attn_ref, g_ref, in_ref, in_got_ref, attn_scale_ref, gain_ref, w_ref,
    grad_attn_ref, grad_mixed_ref, middle_ref, sums_ref,
):
    x = x_ref[...].astype(F32)
    attn = attn_ref[...]
    grad_y = g_ref[...].astype(F32)
    grad_in = in_ref[...] + in_got_ref[...].astype(F32)
    middle = x + attn_scale_ref[...] * attn
    inv = lax.rsqrt(jnp.mean(middle * middle, axis=-1, keepdims=True) + RMS_EPS)
    unit = middle * inv
    scaled = grad_in * gain_ref[...]
    grad_middle = grad_y + inv * (scaled - unit * jnp.mean(scaled * unit, axis=-1, keepdims=True))
    middle_ref[...] = grad_middle
    grad_attn = (attn_scale_ref[...] * grad_middle).astype(BF16)
    grad_attn_ref[...] = grad_attn
    grad_mixed_ref[...] = dot(grad_attn, w_ref[...], NT).astype(BF16)

    @pl.when(pl.program_id(0) == 0)
    def _():
        sums_ref[...] = jnp.zeros_like(sums_ref)

    sums_ref[0:1, :] += jnp.sum(grad_middle * attn, axis=0, keepdims=True)
    sums_ref[1:2, :] += jnp.sum(grad_in * unit, axis=0, keepdims=True)


def join(x, attn, grad_y, grad_in, grad_in_got, attn_scale, gain, w_output):
    rows, width = x.shape
    block = rows // 4
    row = pl.BlockSpec((block, width), lambda i: (i, 0))
    vec = whole((1, width))
    low = jax.ShapeDtypeStruct((rows, width), BF16)
    return pl.pallas_call(
        join_kernel,
        grid=(rows // block,),
        in_specs=[row] * 5 + [vec] * 2 + [whole((width, width))],
        out_specs=[row] * 3 + [whole((8, width))],
        out_shape=[
            low,
            low,
            jax.ShapeDtypeStruct((rows, width), F32),
            jax.ShapeDtypeStruct((8, width), F32),
        ],
        compiler_params=params(1),
        cost_estimate=cost(2 * rows * width * width, rows * width * 22 + 2 * width * width),
        name="join",
    )(x, attn, grad_y, grad_in, grad_in_got, attn_scale, gain, w_output)


def finish_kernel(x_ref, attn_ref, g_ref, out_ref, out_got_ref, attn_scale_ref, mlp_scale_ref, layer_ref, sums_ref):
    down_out = out_ref[...] + out_got_ref[...].astype(F32)
    middle = x_ref[...].astype(F32) + attn_scale_ref[...] * attn_ref[...]
    layer_ref[...] = (middle + mlp_scale_ref[...] * down_out).astype(BF16)

    @pl.when(pl.program_id(0) == 0)
    def _():
        sums_ref[...] = jnp.zeros_like(sums_ref)

    sums_ref[0:1, :] += jnp.sum(g_ref[...].astype(F32) * down_out, axis=0, keepdims=True)


def finish(x, attn, grad_y, out, out_got, attn_scale, mlp_scale):
    rows, width = x.shape
    block = rows // 4
    row = pl.BlockSpec((block, width), lambda i: (i, 0))
    vec = whole((1, width))
    return pl.pallas_call(
        finish_kernel,
        grid=(rows // block,),
        in_specs=[row] * 5 + [vec] * 2,
        out_specs=[row, whole((8, width))],
        out_shape=[
            jax.ShapeDtypeStruct((rows, width), BF16),
            jax.ShapeDtypeStruct((8, width), F32),
        ],
        compiler_params=params(1),
        cost_estimate=cost(8 * rows * width, rows * width * 16),
        name="finish",
    )(x, attn, grad_y, out, out_got, attn_scale, mlp_scale)


def weight_grad_kernel(a_ref, b_ref, out_ref):
    out_ref[...] = dot(a_ref[...], b_ref[...], TN).astype(BF16)


def weight_grad(a, b, name):
    rows, width = a.shape
    columns = b.shape[1]
    block = 512
    return pl.pallas_call(
        weight_grad_kernel,
        grid=(columns // block,),
        in_specs=[whole((rows, width)), pl.BlockSpec((rows, block), lambda j: (0, j))],
        out_specs=pl.BlockSpec((width, block), lambda j: (0, j)),
        out_shape=jax.ShapeDtypeStruct((width, columns), BF16),
        compiler_params=params(1),
        cost_estimate=cost(
            2 * rows * width * columns, 2 * (rows * width + rows * columns + width * columns)
        ),
        name=name,
    )(a, b)


def input_grad_kernel(
    x_ref, gq_ref, gk_ref, gv_ref, middle_ref, gain_ref, wq_ref, wk_ref, wv_ref, out_ref, sums_ref
):
    grad = (
        dot(gq_ref[...], wq_ref[...], NT)
        + dot(gk_ref[...], wk_ref[...], NT)
        + dot(gv_ref[...], wv_ref[...], NT)
    )
    x = x_ref[...].astype(F32)
    centered = x - jnp.mean(x, axis=-1, keepdims=True)
    inv = lax.rsqrt(jnp.mean(centered * centered, axis=-1, keepdims=True) + LN_EPS)
    unit = centered * inv
    scaled = grad * gain_ref[...]
    back = inv * (
        scaled
        - jnp.mean(scaled, axis=-1, keepdims=True)
        - unit * jnp.mean(scaled * unit, axis=-1, keepdims=True)
    )
    out_ref[...] = (middle_ref[...] + back).astype(BF16)

    @pl.when(pl.program_id(0) == 0)
    def _():
        sums_ref[...] = jnp.zeros_like(sums_ref)

    sums_ref[0:1, :] += jnp.sum(grad * unit, axis=0, keepdims=True)


def input_grad(x, gq, gk, gv, grad_middle, gain, w_query, w_key, w_value):
    rows, width = x.shape
    block = rows // 4
    row = pl.BlockSpec((block, width), lambda i: (i, 0))
    square = whole((width, width))
    return pl.pallas_call(
        input_grad_kernel,
        grid=(rows // block,),
        in_specs=[row] * 5 + [whole((1, width))] + [square] * 3,
        out_specs=[row, whole((8, width))],
        out_shape=[
            jax.ShapeDtypeStruct((rows, width), BF16),
            jax.ShapeDtypeStruct((8, width), F32),
        ],
        compiler_params=params(1),
        cost_estimate=cost(2 * 3 * rows * width * width, rows * width * 14 + 6 * width * width),
        name="input_grad",
    )(x, gq, gk, gv, grad_middle, gain, w_query, w_key, w_value)


def log2(n):
    return n.bit_length() - 1


class Places:
    def __init__(self):
        self.n_seq, self.n_sp = lax.axis_size("seq"), lax.axis_size("sp")
        self.sp_bits = log2(self.n_sp)
        self.count = self.sp_bits + log2(self.n_seq)
        self.core = self.sp_bits
        self.me = lax.axis_index("seq") * self.n_sp + lax.axis_index("sp")
        self.down_bits = [b for b in reversed(range(self.count)) if b != self.core]

    def swap(self, value, bit):
        if bit < self.sp_bits:
            axis, size, at = "sp", self.n_sp, bit
        else:
            axis, size, at = "seq", self.n_seq, bit - self.sp_bits
        return lax.ppermute(value, axis, [(i, i ^ (1 << at)) for i in range(size)])

    def own(self, bit):
        return (self.me >> bit) & 1


class Piece:
    def __init__(self, places, value, bits):
        self.places, self.bits = places, list(bits)
        self.value = value.reshape((2,) * len(self.bits) + value.shape[-2:])

    def split(self, value, axis, bit):
        at = self.places.own(bit)
        pick = lambda i: lax.dynamic_index_in_dim(value, i, axis, False)
        return pick(1 - at), pick(at)

    def send(self, bit):
        axis = self.bits.index(bit)
        out, self.value = self.split(self.value, axis, bit)
        self.got = self.places.swap(out, bit)
        self.bits.pop(axis)

    def add(self, low=True):
        self.value = self.value.astype(F32) + self.got.astype(F32)
        if low:
            self.value = self.value.astype(BF16)


def tie(small, pieces):
    small, got = lax.optimization_barrier((small, [p.got for p in pieces]))
    for p, g in zip(pieces, got):
        p.got = g
    return small


def on_device(
    frames, clip_ids, norm_gain, w_query, w_key, w_value, w_output, attn_scale,
    mlp_gain, w_gate, w_up, w_down, mlp_scale, out_grad,
):
    places = Places()
    seqs, length, width = frames.shape
    total_len = clip_ids.shape[1]
    rows = seqs * length
    n_sp, n_seq = places.n_sp, places.n_seq
    devices = n_sp * n_seq
    feed_width = w_gate.shape[1]
    own_rows = width // devices
    feed_rows = feed_width // devices
    block = feed_rows * n_sp
    core = lax.axis_index("seq") & 1
    core_s = core.astype(jnp.int32).reshape(1)
    sp = lax.axis_index("sp")
    sp_bits = list(range(places.core))
    seq_bits = list(range(places.core + 1, places.count))
    flows = ((sp_bits, seq_bits[:1]), (seq_bits[:1], sp_bits))
    late = seq_bits[1:]

    x = frames.reshape(rows, width)
    grad_y = out_grad.reshape(rows, width)

    def neighbours(last, first):
        if n_sp == 2:
            got = lax.ppermute(jnp.where(sp == 0, last, first), "sp", [(0, 1), (1, 0)])
            return got * (sp == 1).astype(got.dtype), got * (sp == 0).astype(got.dtype)
        return (
            lax.ppermute(last, "sp", [(i, i + 1) for i in range(n_sp - 1)]),
            lax.ppermute(first, "sp", [(i + 1, i) for i in range(n_sp - 1)]),
        )

    from_left, from_right = neighbours(frames[:, length - HALF :], frames[:, :HALF])
    grad_y_peer = places.swap(grad_y, places.core)

    start = sp * length
    padded_ids = jnp.pad(clip_ids, ((0, 0), (HALF, HALF)), mode="edge")
    near = lax.dynamic_slice_in_dim(padded_ids, start, length + 2 * HALF, 1)
    first = jnp.sum((clip_ids[:, None, :] < near[:, :, None]).astype(jnp.int32), axis=-1)
    end = jnp.sum((clip_ids[:, None, :] <= near[:, :, None]).astype(jnp.int32), axis=-1)
    frame = lax.broadcasted_iota(jnp.int32, near.shape, 1) + (start - HALF)
    position = (frame - first).astype(F32)
    exponent = jnp.arange(HEAD_DIM // 2, dtype=F32) * (2.0 / HEAD_DIM)
    frequency = jnp.exp(-math.log(10000.0) * exponent)
    angles = position[..., None] * jnp.tile(frequency, LANES // (HEAD_DIM // 2))
    sign = np.where(np.arange(LANES) % HEAD_DIM < HEAD_DIM // 2, -1.0, 1.0).astype(np.float32)
    cos_tab = jnp.cos(angles)
    sin_tab = jnp.sin(angles) * sign
    mid = slice(HALF, HALF + length)
    low = jnp.maximum(frame - HALF, first)[:, mid] - (start - HALF)
    high = jnp.minimum(frame + HALF, end)[:, mid] - (start - HALF)
    padded = -(-length // QB) * QB
    span = jnp.pad(jnp.stack([low, high], axis=1), ((0, 0), (0, 0), (0, padded - length)))

    gain = norm_gain[None]
    normed, query, key, value = project(
        x,
        gain,
        cos_tab[:, mid].reshape(rows, LANES),
        sin_tab[:, mid].reshape(rows, LANES),
        (w_query, w_key, w_value),
    )

    def edges(table):
        return jnp.concatenate([table[:, :HALF], table[:, HALF + length :]], axis=1).reshape(
            seqs * 2 * HALF, -1
        )

    halo = jnp.concatenate([from_left, from_right], axis=1).reshape(seqs * 2 * HALF, width)
    _, key_halo, value_halo = project(
        halo, gain, edges(cos_tab), edges(sin_tab), (w_key, w_value)
    )
    mixed, probs = attend(span, query, key, value, key_halo, value_halo, seqs)

    attn_out, mlp_in = out_proj(mixed, x, w_output, attn_scale[None], mlp_gain[None])
    mlp_in_peer = places.swap(mlp_in, places.core)
    grad_low, grad_hidden = hidden_grad(
        core_s, grad_y, grad_y_peer, mlp_scale[None], w_down, block
    )

    blocks = n_seq // 2
    per = blocks // 2
    every = [b for b in reversed(range(places.count))]

    def start_pair(one, two, bits):
        return [Piece(places, one, bits), Piece(places, two, bits)]

    def go(pair, stage):
        for p, flow in zip(pair, flows):
            for bit in flow[stage][:-1]:
                p.send(bit)
                p.add()
            p.send(flow[stage][-1])

    def land(pair):
        for p in pair:
            p.add()

    *kept, gate_one, up_one = feed(
        core_s, mlp_in, mlp_in_peer, grad_hidden, w_gate, w_up, block, 0, per, ()
    )

    def rows_pair(one, two, bits):
        return start_pair(one, two, bits)

    def by_bits(value, rows_each):
        return value.reshape(-1, rows_each, value.shape[-1])

    first = rows_pair(by_bits(gate_one, own_rows), by_bits(up_one, own_rows), every)
    go(first, 0)
    *kept, gate_two, up_two = feed(
        core_s, mlp_in, mlp_in_peer, grad_hidden, w_gate, w_up, block, per, per, tuple(kept)
    )
    hidden, grad_gate, grad_up = kept
    small = tie(core_s, first)
    land(first)
    go(first, 1)
    second = rows_pair(by_bits(gate_two, own_rows), by_bits(up_two, own_rows), every)
    go(second, 0)

    in_peer = feed_back(small, (grad_gate, grad_up), (w_gate, w_up), block, 1, BF16)
    in_got = places.swap(in_peer, places.core)
    in_own = feed_back(small, (grad_gate, grad_up), (w_gate, w_up), block, 0, F32)
    down_one, down_two = down(hidden, grad_low)
    scale_row = tie(attn_scale[None], first + second)
    land(first)
    land(second)
    go(second, 1)
    third = rows_pair(by_bits(down_one, feed_rows), by_bits(down_two, feed_rows), places.down_bits)
    go(third, 0)

    grad_attn, grad_mixed, grad_middle, join_sums = join(
        x, attn_out, grad_y, in_own, in_got, scale_row, mlp_gain[None], w_output
    )
    grad_query, grad_key, grad_value, key_edge, value_edge = attend_back(
        probs, query, key, value, key_halo, value_halo, grad_mixed, cos_tab, sin_tab, seqs
    )
    edge = jnp.concatenate([key_edge, value_edge], axis=1).reshape(seqs, 2 * HALF, 2 * width)
    to_right, to_left = neighbours(edge[:, HALF:], edge[:, :HALF])

    def with_edges(own, at):
        own = own.reshape(seqs, length, width)
        left = own[:, :HALF] + to_right[..., at * width : (at + 1) * width]
        right = own[:, length - HALF :] + to_left[..., at * width : (at + 1) * width]
        return jnp.concatenate([left, own[:, HALF : length - HALF], right], axis=1).reshape(
            rows, width
        )

    fourth = rows_pair(
        by_bits(weight_grad(mixed, grad_attn, "output_weight"), own_rows),
        by_bits(weight_grad(normed, grad_query, "query_weight"), own_rows),
        every,
    )
    for p in fourth:
        p.send(places.core)
    scale_row = tie(gain, second + third + fourth)
    land(second)
    land(third)
    land(fourth)
    go(third, 1)
    go(fourth, 0)

    grad_key = with_edges(grad_key, 0)
    grad_value = with_edges(grad_value, 1)
    frames_grad, norm_sums = input_grad(
        x, grad_query, grad_key, grad_value, grad_middle, scale_row, w_query, w_key, w_value
    )
    fifth = rows_pair(
        by_bits(weight_grad(normed, grad_key, "key_weight"), own_rows),
        by_bits(weight_grad(normed, grad_value, "value_weight"), own_rows),
        every,
    )
    for p in fifth:
        p.send(places.core)

    small = tie(core_s, third + fourth)
    land(third)
    land(fourth)
    go(fourth, 1)
    out_peer = feed_out(small, hidden, w_down, block, 1, BF16)
    out_got = places.swap(out_peer, places.core)
    small = tie(small, fifth)
    land(fifth)
    go(fifth, 0)
    out_own = feed_out(small, hidden, w_down, block, 0, F32)
    layer_out, out_sums = finish(
        x, attn_out, grad_y, out_own, out_got, attn_scale[None], mlp_scale[None]
    )
    land(fourth)
    land(fifth)
    go(fifth, 1)
    land(fifth)

    def rest(pairs):
        joined = Piece(places, jnp.concatenate([p.value for pair in pairs for p in pair], axis=-1), pairs[0][0].bits)
        for bit in late:
            joined.send(bit)
            joined.add(bit != late[-1])
        return joined.value

    feeds = rest([first, second])
    downs = rest([third])
    one = rest([fourth])
    two = rest([fifth])
    output_grad, query_grad = one[:, :width], one[:, width:]
    key_grad, value_grad = two[:, :width], two[:, width:]

    vectors = jnp.stack([norm_sums[0], join_sums[0], join_sums[1], out_sums[0]], axis=1)
    piece = Piece(places, by_bits(vectors, own_rows), every)
    for bit in [places.core] + sp_bits + seq_bits:
        piece.send(bit)
        piece.add(False)
    vectors = piece.value.T

    wide = per * block
    halves = feeds.reshape(2, own_rows, 2, 2, wide).transpose(0, 1, 3, 2, 4)
    halves = halves.reshape(2, own_rows, 2 * blocks * block)
    mine = lax.dynamic_index_in_dim(halves, core, 0, False)
    got = places.swap(lax.dynamic_index_in_dim(halves, 1 - core, 0, False), places.core)
    pair = jnp.stack([jnp.where(core == 0, mine, got), jnp.where(core == 0, got, mine)], axis=0)
    pair = pair.reshape(2, own_rows, 2, blocks, block)
    pair = pair.transpose(2, 1, 3, 0, 4).reshape(2, own_rows, feed_width)
    return (
        layer_out.reshape(frames.shape),
        frames_grad.reshape(frames.shape),
        vectors[0],
        query_grad,
        key_grad,
        value_grad,
        output_grad,
        vectors[1],
        vectors[2],
        pair[0],
        pair[1],
        downs,
        vectors[3],
    )


def solution(mesh):
    split = P("seq", "sp", None)
    rows = P(("seq", "sp"), None)
    vec = P(("seq", "sp"))
    return jax.shard_map(
        on_device,
        mesh=mesh,
        in_specs=(split, P("seq", None)) + (P(),) * 11 + (split,),
        out_specs=(
            split, split, vec, rows, rows, rows, rows, vec, vec, rows, rows, rows, vec,
        ),
        check_vma=False,
    )
```

time: 1910 us -> 440 us (0.23)
  waiting for transfers between devices: 631 us -> 52.6 us
  local copies, waits for them, and re-layouts: 518 us -> 59.4 us
  matrix products: 380 us -> 0 us
  other arithmetic: 303 us -> 46.2 us
  Pallas kernels: 0 us -> 231 us
    reduce_scatter x1 -> x0, waiting for transfers between devices: 600 us -> none  [on_device(): lax.psum_scatter(jnp.concatenate([jnp.concatenate([query_part, key_part,...]
    dot_general x35 -> x0, matrix products: 380 us -> none  [the longest x4 75 us: one_block(): jnp.einsum('snqhd,snkhd->snhqk', query_blk, key_blk, preferred_element_ty...]
    pallas_call x0 -> x20, Pallas kernels: none -> 231 us  [the longest x2 43.7 us: feed(): pl.pallas_call(feed_kernel, grid_spec=pltpu.PrefetchScalarGridSpec(num_sc...]
    unnamed x11 -> x1, other arithmetic: 203 us -> 0.71 us
    dynamic_update_slice x8 -> x0, local copies, waits for them, and re-layouts: 115 us -> none  [the longest x4 73.9 us: attend_backward(): lax.scan(one_block, (zero_pad, zero_pad), jnp.arange(rows_all // block_ro...]
    concatenate x1, local copies, waits for them, and re-layouts: 96.2 us -> 0.8 us  [on_device(): padded_ids = jnp.pad(clip_ids, ((0, 0), (HALF, HALF)), mode='edge')]
    unnamed x131 -> x77, local copies, waits for them, and re-layouts: 99.8 us -> 6.8 us
    all_to_all x12 -> x0, local copies, waits for them, and re-layouts: 60.3 us -> none  [the longest x2 13.8 us: on_device(): lax.all_to_all(value_time.reshape(seqs, local_len, width), 'sp', split_ax...]
  transfers between devices with their start and end apart: 9 -> 44, of which waited for: 5 -> 8; matrix products, arithmetic and copies ran while one was open for 18% -> 22% of each run, Pallas kernels for 0% -> 48%
where the time goes in v1:
time: 440 us; the launch traced here: 435 us
  Pallas kernels  231 us (52%)
  local copies, waits for them, and re-layouts  59.4 us (14%)
  waiting for transfers between devices  52.6 us (12%)
  other arithmetic  46.2 us (10%)
  starting transfers between devices  43.9 us (10%)
    ppermute x42, waiting for transfers between devices, swap(): return lax.ppermute(value, axis, [(i, i ^ 1 << at) for i in range(size)])  52.6 us
    pallas_call x2, Pallas kernels, feed(): pl.pallas_call(feed_kernel, grid_spec=pltpu.PrefetchScalarGridSpec(num_sc...  43.7 us
    ppermute x42, starting transfers between devices, swap(): return lax.ppermute(value, axis, [(i, i ^ 1 << at) for i in range(size)])  39.9 us
    convert_element_type x28, other arithmetic, add(): self.value = self.value.astype(BF16)  28.9 us
    dynamic_slice x22, local copies, waits for them, and re-layouts, split(): pick = lambda i: lax.dynamic_index_in_dim(value, i, axis, False)  27.6 us
    pallas_call x2, Pallas kernels, feed_back(): pl.pallas_call(feed_back_kernel, grid_spec=pltpu.PrefetchScalarGridSpec(n...  25.7 us
    pallas_call x2, Pallas kernels, project(): pl.pallas_call(functools.partial(project_kernel, with_query), grid=(grid,...  24.4 us
    pallas_call x4, Pallas kernels, weight_grad(): pl.pallas_call(weight_grad_kernel, grid=(columns // block,), in_specs=[wh...  21.4 us
  transfers between devices with their start and end apart: 44, of which 8 were waited for; matrix products, arithmetic and copies ran while one was open for 22% of the time, Pallas kernels for 48%

profile of v1, /device:TPU:0, one launch (start us, length us, event | category | flops | bytes accessed | tf_op | source)
XLA Modules:
  0.0 434.7 jit_solution(4854906560594148921)
XLA Ops:
  1.6 3.0 collective-permute-start
  5.4 1.3 fusion.63
  8.9 1.4 convert_reduce_fusion.1
  10.3 2.4 fusion.32
  14.6 17.0 %project_rows.1 = (bf16[832,1024]{1,0:T(8,128)(2,1)}, bf16[832,1024]{1,0:T(8,128)(2,1)}, bf16[832,1024]{1,0:T(8,128)(2,1)}, bf16[832,1024]{1,0:T(8,128)(2,1)}) custom-call(bf16[832,1024]{1,0:T(8,128)(2,1)} %bitcast.297, f32[1,1024]{1,0:T(1,128)} %bitcast.336, f32[832,128]{1,0:T(8,128)} %get-tuple-element.192.cos_ref, f32[832,128]{1,0:T(8,128)} %get-tuple-element.191.sin_ref, ...), custom_call_target="tpu_custom_call" | custom-call | flops 5234491392 | bytes 14811136 | tf_op jit(solution)/shard_map/project_rows/pallas_call | solution.py:99
  33.6 7.4 %project_halo.1 = (bf16[128,1024]{1,0:T(8,128)(2,1)}, bf16[128,1024]{1,0:T(8,128)(2,1)}, bf16[128,1024]{1,0:T(8,128)(2,1)}) custom-call(bf16[128,1024]{1,0:T(8,128)(2,1)} %maximum_bitcast_fusion.4.x_ref, f32[1,1024]{1,0:T(1,128)} %bitcast.337, f32[128,128]{1,0:T(8,128)} %maximum_bitcast_fusion.5.cos_ref, f32[128,128]{1,0:T(8,128)} %maximum_bitcast_fusion.6.sin_ref, ...), custom_call_target="tpu_custom_call" | custom-call | flops 536870912 | bytes 5242880 | tf_op jit(solution)/shard_map/project_halo/pallas_call | solution.py:99
  41.0 15.5 %attend.1 = (bf16[832,1024]{1,0:T(8,128)(2,1)}, bf16[256,14336]{1,0:T(8,128)(2,1)}) custom-call(s32[1,2,896]{2,1,0:T(2,128)} %pad.4.span_ref, bf16[832,1024]{1,0:T(8,128)(2,1)} %get-tuple-element.73.q_ref, bf16[832,1024]{1,0:T(8,128)(2,1)} %get-tuple-element.74.k_ref, bf16[832,1024]{1,0:T(8,128)(2,1)} %get-tuple-element.75.v_ref, ...), custom_call_target="tpu_custom_call" | custom-call | flops 3758096384 | bytes 14155776 | tf_op jit(solution)/shard_map/attend/pallas_call | solution.py:179
  56.5 6.7 %out_proj.1 = (f32[832,1024]{1,0:T(8,128)}, bf16[832,1024]{1,0:T(8,128)(2,1)}) custom-call(bf16[832,1024]{1,0:T(8,128)(2,1)} %get-tuple-element.78.m_ref.a_ref, bf16[832,1024]{1,0:T(8,128)(2,1)} %bitcast.298, bf16[1024,1024]{1,0:T(8,128)(2,1)} %w_ref.5, f32[1,1024]{1,0:T(1,128)} %bitcast.327, f32[1,1024]{1,0:T(1,128)} %bitcast.333), custom_call_target="tpu_custom_call" | custom-call | flops 1744830464 | bytes 10616832 | tf_op jit(solution)/shard_map/out_proj/pallas_call | solution.py:316
  64.9 13.5 %hidden_grad.1 = (bf16[1664,1024]{1,0:T(8,128)(2,1)}, bf16[1664,2048]{1,0:T(8,128)(2,1)}) custom-call(s32[1]{0:T(128)} %bitcast.17.core_ref, bf16[832,1024]{1,0:T(8,128)(2,1)} %bitcast.303, bf16[832,1024]{1,0:T(8,128)(2,1)} %copy-done.35, f32[1,1024]{1,0:T(1,128)} %bitcast.331, bf16[4096,1024]{1,0:T(8,128)(2,1)} %two_ref.3), custom_call_target="tpu_custom_call" | custom-call | flops 6979321856 | bytes 17825792 | tf_op jit(solution)/shard_map/hidden_grad/pallas_call | solution.py:346
  78.4 22.0 %feed.2 = (bf16[1664,2048]{1,0:T(8,128)(2,1)}, bf16[1664,2048]{1,0:T(8,128)(2,1)}, bf16[1664,2048]{1,0:T(8,128)(2,1)}, bf16[1024,1024]{1,0:T(8,128)(2,1)}, bf16[1024,1024]{1,0:T(8,128)(2,1)}) custom-call(s32[1]{0:T(128)} %bitcast.17.core_ref, bf16[832,1024]{1,0:T(8,128)(2,1)} %get-tuple-element.80.xo_ref, bf16[832,1024]{1,0:T(8,128)(2,1)} %collective-permute-done.1.xp_ref, ...), custom_call_target="tpu_custom_call" | custom-call | flops 13958643712 | bytes 28835840 | tf_op jit(solution)/shard_map/feed/pallas_call | solution.py:405
  100.4 1.7 constant_dynamic-slice_fusion.27
  105.4 1.5 collective-permute-start.4
  106.9 21.8 %feed.3 = (bf16[1664,2048]{1,0:T(8,128)(2,1)}, bf16[1664,2048]{1,0:T(8,128)(2,1)}, bf16[1664,2048]{1,0:T(8,128)(2,1)}, bf16[1024,1024]{1,0:T(8,128)(2,1)}, bf16[1024,1024]{1,0:T(8,128)(2,1)}) custom-call(s32[1]{0:T(128)} %bitcast.17.core_ref, bf16[832,1024]{1,0:T(8,128)(2,1)} %get-tuple-element.80.xo_ref, ...), custom_call_target="tpu_custom_call", output_to_operand_aliasing={{0}: (6, {}), {1}: (7, {}), {2}: (8, {})} | custom-call | flops 13958643712 | bytes 28835840 | tf_op jit(solution)/shard_map/feed/pallas_call | solution.py:405
  128.6 1.8 constant_dynamic-slice_fusion.28
  134.5 12.1 %down_weight.1 = (bf16[2048,512]{1,0:T(8,128)(2,1)}, bf16[2048,512]{1,0:T(8,128)(2,1)}) custom-call(bf16[1664,2048]{1,0:T(8,128)(2,1)} %get-tuple-element.85.hid_ref, bf16[1664,1024]{1,0:T(8,128)(2,1)} %get-tuple-element.86.low_ref), custom_call_target="tpu_custom_call" | custom-call | flops 6979321856 | bytes 14417920 | tf_op jit(solution)/shard_map/down_weight/pallas_call | solution.py:437
  146.6 2.8 constant_dynamic-slice_fusion.29
  154.6 1.6 fusion.8
  157.1 1.5 collective-permute-start.5
  158.6 1.6 fusion.7
  161.3 12.5 %feed_back.3 = bf16[832,1024]{1,0:T(8,128)(2,1)} custom-call(s32[1]{0:T(128)} %bitcast.17.core_ref, bf16[1664,2048]{1,0:T(8,128)(2,1)} %get-tuple-element.98.refs_0_, bf16[1664,2048]{1,0:T(8,128)(2,1)} %get-tuple-element.99.refs_1_, bf16[1024,4096]{1,0:T(8,128)(2,1)} %refs_3_.3, bf16[1024,4096]{1,0:T(8,128)(2,1)} %refs_3_.3, bf16[1024,4096]{1,0:T(8,128)(2,1)} %refs_5_.3, ...), custom_call_target="tpu_custom_call" | custom-call | flops 6979321856 | bytes 15204352 | tf_op jit(solution)/shard_map/feed_back/pallas_call | solution.py:481
  173.8 13.2 %feed_back.2.in_ref = f32[832,1024]{1,0:T(8,128)} custom-call(s32[1]{0:T(128)} %bitcast.17.core_ref, bf16[1664,2048]{1,0:T(8,128)(2,1)} %get-tuple-element.98.refs_0_, bf16[1664,2048]{1,0:T(8,128)(2,1)} %get-tuple-element.99.refs_1_, bf16[1024,4096]{1,0:T(8,128)(2,1)} %refs_3_.3, bf16[1024,4096]{1,0:T(8,128)(2,1)} %refs_3_.3, bf16[1024,4096]{1,0:T(8,128)(2,1)} %refs_5_.3, ...), custom_call_target="tpu_custom_call" | custom-call | flops 6979321856 | bytes 15204352 | tf_op jit(solution)/shard_map/feed_back/pallas_call | solution.py:481
  188.6 1.8 fusion.9
  191.4 1.5 collective-permute-start.9
  192.9 1.6 fusion.6
  197.7 10.8 %join.1 = (bf16[832,1024]{1,0:T(8,128)(2,1)}, bf16[832,1024]{1,0:T(8,128)(2,1)}, f32[832,1024]{1,0:T(8,128)}, f32[8,1024]{1,0:T(8,128)}) custom-call(bf16[832,1024]{1,0:T(8,128)(2,1)} %bitcast.299, f32[832,1024]{1,0:T(8,128)} %get-tuple-element.79.attn_ref, bf16[832,1024]{1,0:T(8,128)(2,1)} %bitcast.304, f32[832,1024]{1,0:T(8,128)} %feed_back.2.in_ref, ...), custom_call_target="tpu_custom_call" | custom-call | flops 1744830464 | bytes 20840448 | tf_op jit(solution)/shard_map/join/pallas_call | solution.py:573
  208.5 5.3 %output_weight.1 = bf16[1024,1024]{1,0:T(8,128)(2,1)} custom-call(bf16[832,1024]{1,0:T(8,128)(2,1)} %get-tuple-element.78.m_ref.a_ref, bf16[832,1024]{1,0:T(8,128)(2,1)} %get-tuple-element.101.b_ref), custom_call_target="tpu_custom_call" | custom-call | flops 1744830464 | bytes 5505024 | tf_op jit(solution)/shard_map/output_weight/pallas_call | solution.py:630
  213.8 2.7 constant_dynamic-slice_fusion.15
  217.6 18.5 %attend_back.1 = (bf16[832,1024]{1,0:T(8,128)(2,1)}, bf16[832,1024]{1,0:T(8,128)(2,1)}, bf16[832,1024]{1,0:T(8,128)(2,1)}, bf16[128,1024]{1,0:T(8,128)(2,1)}, bf16[128,1024]{1,0:T(8,128)(2,1)}) custom-call(bf16[256,14336]{1,0:T(8,128)(2,1)} %get-tuple-element.103.p_ref, bf16[832,1024]{1,0:T(8,128)(2,1)} %get-tuple-element.73.q_ref, ...), custom_call_target="tpu_custom_call" | custom-call | flops 7516192768 | bytes 20971520 | tf_op jit(solution)/shard_map/attend_back/pallas_call | solution.py:270
  238.8 5.3 %query_weight.1 = bf16[1024,1024]{1,0:T(8,128)(2,1)} custom-call(bf16[832,1024]{1,0:T(8,128)(2,1)} %get-tuple-element.102.a_ref, bf16[832,1024]{1,0:T(8,128)(2,1)} %get-tuple-element.105.b_ref.gq_ref), custom_call_target="tpu_custom_call" | custom-call | flops 1744830464 | bytes 5505024 | tf_op jit(solution)/shard_map/query_weight/pallas_call | solution.py:630
  244.2 2.8 constant_dynamic-slice_fusion.14
  253.2 1.3 maximum_bitcast_fusion.b_ref.gk_ref
  254.5 5.4 %key_weight.1 = bf16[1024,1024]{1,0:T(8,128)(2,1)} custom-call(bf16[832,1024]{1,0:T(8,128)(2,1)} %get-tuple-element.102.a_ref, bf16[832,1024]{1,0:T(8,128)(2,1)} %maximum_bitcast_fusion.b_ref.gk_ref), custom_call_target="tpu_custom_call" | custom-call | flops 1744830464 | bytes 5505024 | tf_op jit(solution)/shard_map/key_weight/pallas_call | solution.py:630
  261.1 1.7 constant_dynamic-slice_fusion.1
  263.9 1.3 maximum_bitcast_fusion.1.b_ref.gv_ref
  265.2 5.3 %value_weight.1 = bf16[1024,1024]{1,0:T(8,128)(2,1)} custom-call(bf16[832,1024]{1,0:T(8,128)(2,1)} %get-tuple-element.102.a_ref, bf16[832,1024]{1,0:T(8,128)(2,1)} %maximum_bitcast_fusion.1.b_ref.gv_ref), custom_call_target="tpu_custom_call" | custom-call | flops 1744830464 | bytes 5505024 | tf_op jit(solution)/shard_map/value_weight/pallas_call | solution.py:630
  270.5 1.7 constant_dynamic-slice_fusion
  274.1 2.1 fusion.10
  277.8 1.6 fusion.5
  281.5 1.6 fusion.4
  284.9 15.0 %input_grad.1 = (bf16[832,1024]{1,0:T(8,128)(2,1)}, f32[8,1024]{1,0:T(8,128)}) custom-call(bf16[832,1024]{1,0:T(8,128)(2,1)} %bitcast.300, bf16[832,1024]{1,0:T(8,128)(2,1)} %get-tuple-element.105.b_ref.gq_ref, bf16[832,1024]{1,0:T(8,128)(2,1)} %maximum_bitcast_fusion.b_ref.gk_ref, bf16[832,1024]{1,0:T(8,128)(2,1)} %maximum_bitcast_fusion.1.b_ref.gv_ref, ...), custom_call_target="tpu_custom_call" | custom-call | flops 5234491392 | bytes 18219008 | tf_op jit(solution)/shard_map/input_grad/pallas_call | solution.py:676
  300.8 1.5 fusion.14
  305.6 1.6 collective-permute-start.19
  308.3 1.6 collective-permute-start.39
  309.9 8.8 %collective-permute-done.19 = bf16[2,2,2,32,1024]{4,3,0,1,2:T(8,128)(2,1)S(1)} collective-permute-done((bf16[2,2,2,32,1024]{4,3,0,1,2:T(8,128)(2,1)S(1)}, bf16[2,2,2,32,1024]{4,3,0,1,2:T(8,128)(2,1)S(1)}, u32[]{:S(2)}, u32[]{:S(2)}) %collective-permute-start.19) | collective-permute-done | bytes 524320 | tf_op jit(solution)/shard_map/ppermute | solution.py:709
  318.7 8.1 %feed_out.3 = bf16[832,1024]{1,0:T(8,128)(2,1)} custom-call(s32[1]{0:T(128)} %bitcast.17.core_ref, bf16[1664,2048]{1,0:T(8,128)(2,1)} %get-tuple-element.85.hid_ref, bf16[4096,1024]{1,0:T(8,128)(2,1)} %two_ref.3, bf16[4096,1024]{1,0:T(8,128)(2,1)} %two_ref.3), custom_call_target="tpu_custom_call" | custom-call | flops 3489660928 | bytes 7602176 | tf_op jit(solution)/shard_map/feed_out/pallas_call | solution.py:521
  326.8 1.3 fusion.21
  328.2 1.6 collective-permute-start.29
  331.0 1.7 fusion.2
  335.9 1.6 fusion.1
  341.8 1.6 collective-permute-start.31
  343.4 8.7 %feed_out.2.out_ref = f32[832,1024]{1,0:T(8,128)} custom-call(s32[1]{0:T(128)} %bitcast.17.core_ref, bf16[1664,2048]{1,0:T(8,128)(2,1)} %get-tuple-element.85.hid_ref, bf16[4096,1024]{1,0:T(8,128)(2,1)} %two_ref.3, bf16[4096,1024]{1,0:T(8,128)(2,1)} %two_ref.3), custom_call_target="tpu_custom_call" | custom-call | flops 3489660928 | bytes 7602176 | tf_op jit(solution)/shard_map/feed_out/pallas_call | solution.py:521
  352.7 2.7 collective-permute-start.32
  356.6 1.6 collective-permute-start.34
  360.4 1.5 fusion
  362.0 6.0 %collective-permute-done.42 = bf16[2,128,1024]{2,1,0:T(8,128)(2,1)S(1)} collective-permute-done((bf16[2,128,1024]{2,1,0:T(8,128)(2,1)}, bf16[2,128,1024]{2,1,0:T(8,128)(2,1)S(1)}, u32[]{:S(2)}, u32[]{:S(2)}) %collective-permute-start.42) | collective-permute-done | bytes 524320 | tf_op jit(solution)/shard_map/ppermute | solution.py:709
  369.4 1.8 collective-permute-start.43
  372.4 31.3 %collective-permute-done.43 = bf16[128,1024]{1,0:T(8,128)(2,1)S(1)} collective-permute-done((bf16[128,1024]{1,0:T(8,128)(2,1)S(1)}, bf16[128,1024]{1,0:T(8,128)(2,1)S(1)}, u32[]{:S(2)}, u32[]{:S(2)}) %collective-permute-start.43) | collective-permute-done | bytes 262176 | tf_op jit(solution)/shard_map/ppermute | solution.py:709
  407.4 6.7 %finish.1 = (bf16[832,1024]{1,0:T(8,128)(2,1)}, f32[8,1024]{1,0:T(8,128)}) custom-call(bf16[832,1024]{1,0:T(8,128)(2,1)} %bitcast.301, f32[832,1024]{1,0:T(8,128)} %get-tuple-element.79.attn_ref, bf16[832,1024]{1,0:T(8,128)(2,1)} %bitcast.305, f32[832,1024]{1,0:T(8,128)} %feed_out.2.out_ref, bf16[832,1024]{1,0:T(8,128)(2,1)} %collective-permute-done.23.out_got_ref, ...), custom_call_target="tpu_custom_call" | custom-call | flops 6815744 | bytes 13631488 | tf_op jit(solution)/shard_map/finish/pallas_call | solution.py:607
  418.2 2.1 collective-permute-done.25
  420.3 1.6 collective-permute-start.26
  422.3 1.7 collective-permute-done.26
  424.0 2.1 collective-permute-start.27
  426.2 1.5 collective-permute-done.27
  427.7 2.8 collective-permute-start.28
  (260 shorter events, 81.5 us)
Async XLA Ops:
  1.6 31.2 %collective-permute-start = (bf16[1,64,1024]{2,1,0:T(8,128)(2,1)S(1)}, bf16[1,64,1024]{2,1,0:T(8,128)(2,1)S(1)}, u32[]{:S(2)}, u32[]{:S(2)}) collective-permute-start(bf16[1,64,1024]{2,1,0:T(8,128)(2,1)S(1)} %slice_select_fusion.1), channel_id=1, source_target_pairs={{0,1},{1,0},{2,3},{3,2},{4,5},{5,4},{6,7},{7,6},{8,9},{9,8},{10,11... | collective-permute-start | bytes 393224 | tf_op jit(solution)/shard_map/ppermute | solution.py:771
  4.6 59.1 %collective-permute-start.2 = (bf16[832,1024]{1,0:T(8,128)(2,1)}, bf16[832,1024]{1,0:T(8,128)(2,1)S(1)}, u32[]{:S(2)}, u32[]{:S(2)}) collective-permute-start(bf16[832,1024]{1,0:T(8,128)(2,1)} %bitcast.302), channel_id=1, source_target_pairs={{0,2},{2,0},{4,6},{6,4},{8,10},{10,8},{12,14},{14,12},{16,18},{18,... | collective-permute-start | bytes 5111816 | tf_op jit(solution)/shard_map/ppermute | solution.py:709
  12.8 18.8 %copy-start.20 = (f32[1,960,128]{2,1,0:T(8,128)}, f32[1,960,128]{2,1,0:T(8,128)S(1)}, u32[]{:S(2)}) copy-start(f32[1,960,128]{2,1,0:T(8,128)S(1)} %get-tuple-element.183.sin_ref) | copy-start | bytes 1474564
  12.8 18.8 %copy-start.21 = (f32[1,960,128]{2,1,0:T(8,128)}, f32[1,960,128]{2,1,0:T(8,128)S(1)}, u32[]{:S(2)}) copy-start(f32[1,960,128]{2,1,0:T(8,128)S(1)} %get-tuple-element.184.cos_ref) | copy-start | bytes 1474564
  63.2 15.2 %collective-permute-start.1 = (bf16[832,1024]{1,0:T(8,128)(2,1)}, bf16[832,1024]{1,0:T(8,128)(2,1)}, u32[]{:S(2)}, u32[]{:S(2)}) collective-permute-start(bf16[832,1024]{1,0:T(8,128)(2,1)} %get-tuple-element.80.xo_ref), channel_id=1, source_target_pairs={{0,2},{2,0},{4,6},{6,4},{8,10},{10,8},{12,14},{14,12},{16,18},{18,... | collective-permute-start | bytes 5111816 | tf_op jit(solution)/shard_map/ppermute | solution.py:709
  103.2 50.4 %collective-permute-start.3 = (bf16[2,2,2,2,32,1024]{5,4,3,0,1,2:T(8,128)(2,1)}, bf16[2,2,2,2,32,1024]{5,4,3,0,1,2:T(8,128)(2,1)S(1)}, u32[]{:S(2)}, u32[]{:S(2)}) collective-permute-start(bf16[2,2,2,2,32,1024]{5,4,3,0,1,2:T(8,128)(2,1)} %bitcast.295), channel_id=1, source_target_pairs={{0,1},{1,0},{2,3},{3,2},{4,5},{5,4},{6,7},{7,6},{8,9},{9,8},{10,11... | collective-permute-start | bytes 3145736 | tf_op jit(solution)/shard_map/ppermute | solution.py:709
  105.4 48.2 %collective-permute-start.4 = (bf16[2,2,2,2,32,1024]{5,4,2,0,1,3:T(8,128)(2,1)}, bf16[2,2,2,2,32,1024]{5,4,2,0,1,3:T(8,128)(2,1)}, u32[]{:S(2)}, u32[]{:S(2)}) collective-permute-start(bf16[2,2,2,2,32,1024]{5,4,2,0,1,3:T(8,128)(2,1)} %bitcast.294), channel_id=1, source_target_pairs={{0,4},{2,6},{4,0},{6,2},{8,12},{10,14},{12,8},{14,10},{16,20},{18,... | collective-permute-start | bytes 3145736 | tf_op jit(solution)/shard_map/ppermute | solution.py:709
  131.6 55.4 %collective-permute-start.7 = (bf16[2,2,2,2,32,1024]{5,4,3,0,1,2:T(8,128)(2,1)}, bf16[2,2,2,2,32,1024]{5,4,3,0,1,2:T(8,128)(2,1)}, u32[]{:S(2)}, u32[]{:S(2)}) collective-permute-start(bf16[2,2,2,2,32,1024]{5,4,3,0,1,2:T(8,128)(2,1)} %bitcast.293), channel_id=1, source_target_pairs={{0,1},{1,0},{2,3},{3,2},{4,5},{5,4},{6,7},{7,6},{8,9},{9,8},{10,11... | collective-permute-start | bytes 3145736 | tf_op jit(solution)/shard_map/ppermute | solution.py:709
  134.0 54.1 %collective-permute-start.8 = (bf16[2,2,2,2,32,1024]{5,4,2,0,1,3:T(8,128)(2,1)}, bf16[2,2,2,2,32,1024]{5,4,2,0,1,3:T(8,128)(2,1)}, u32[]{:S(2)}, u32[]{:S(2)}) collective-permute-start(bf16[2,2,2,2,32,1024]{5,4,2,0,1,3:T(8,128)(2,1)} %bitcast.292), channel_id=1, source_target_pairs={{0,4},{2,6},{4,0},{6,2},{8,12},{10,14},{12,8},{14,10},{16,20},{18,... | collective-permute-start | bytes 3145736 | tf_op jit(solution)/shard_map/ppermute | solution.py:709
  157.1 31.5 %collective-permute-start.5 = (bf16[2,2,2,32,1024]{4,3,2,0,1:T(8,128)(2,1)}, bf16[2,2,2,32,1024]{4,3,2,0,1:T(8,128)(2,1)S(1)}, u32[]{:S(2)}, u32[]{:S(2)}) collective-permute-start(bf16[2,2,2,32,1024]{4,3,2,0,1:T(8,128)(2,1)} %dynamic-slice_bitcast_fusion.12), channel_id=1, source_target_pairs={{0,4},{2,6},{4,0},{6,2},{8,12},{10,14},{12,8},{14,10},{16,20},{18,... | collective-permute-start | bytes 1572872 | tf_op jit(solution)/shard_map/ppermute | solution.py:709
  160.3 28.3 %collective-permute-start.6 = (bf16[2,2,2,32,1024]{4,3,2,0,1:T(8,128)(2,1)S(1)}, bf16[2,2,2,32,1024]{4,3,2,0,1:T(8,128)(2,1)S(1)}, u32[]{:S(2)}, u32[]{:S(2)}) collective-permute-start(bf16[2,2,2,32,1024]{4,3,2,0,1:T(8,128)(2,1)S(1)} %dynamic-slice_bitcast_fusion.11), channel_id=1, source_target_pairs={{0,1},{1,0},{2,3},{3,2},{4,5},{5,4},{6,7},{7,6},{8,9},{9,8},{10,11... | collective-permute-start | bytes 1572872 | tf_op jit(solution)/shard_map/ppermute | solution.py:709
  173.8 23.9 %collective-permute-start.13 = (bf16[832,1024]{1,0:T(8,128)(2,1)}, bf16[832,1024]{1,0:T(8,128)(2,1)}, u32[]{:S(2)}, u32[]{:S(2)}) collective-permute-start(bf16[832,1024]{1,0:T(8,128)(2,1)} %feed_back.3), channel_id=1, source_target_pairs={{0,2},{2,0},{4,6},{6,4},{8,10},{10,8},{12,14},{14,12},{16,18},{18,... | collective-permute-start | bytes 5111816 | tf_op jit(solution)/shard_map/ppermute | solution.py:709
  187.0 72.9 %collective-permute-start.11 = (bf16[2,2,2,128,512]{4,3,0,1,2:T(8,128)(2,1)}, bf16[2,2,2,128,512]{4,3,0,1,2:T(8,128)(2,1)}, u32[]{:S(2)}, u32[]{:S(2)}) collective-permute-start(bf16[2,2,2,128,512]{4,3,0,1,2:T(8,128)(2,1)} %bitcast.291), channel_id=1, source_target_pairs={{0,1},{1,0},{2,3},{3,2},{4,5},{5,4},{6,7},{7,6},{8,9},{9,8},{10,11... | collective-permute-start | bytes 3145736 | tf_op jit(solution)/shard_map/ppermute | solution.py:709
  188.1 85.2 %collective-permute-start.12 = (bf16[2,2,2,128,512]{4,3,0,1,2:T(8,128)(2,1)}, bf16[2,2,2,128,512]{4,3,0,1,2:T(8,128)(2,1)}, u32[]{:S(2)}, u32[]{:S(2)}) collective-permute-start(bf16[2,2,2,128,512]{4,3,0,1,2:T(8,128)(2,1)} %bitcast.290), channel_id=1, source_target_pairs={{0,4},{2,6},{4,0},{6,2},{8,12},{10,14},{12,8},{14,10},{16,20},{18,... | collective-permute-start | bytes 3145736 | tf_op jit(solution)/shard_map/ppermute | solution.py:709
  190.4 4.1 copy-start.4
  191.4 81.9 %collective-permute-start.9 = (bf16[2,2,2,32,1024]{4,3,2,0,1:T(8,128)(2,1)}, bf16[2,2,2,32,1024]{4,3,2,0,1:T(8,128)(2,1)S(1)}, u32[]{:S(2)}, u32[]{:S(2)}) collective-permute-start(bf16[2,2,2,32,1024]{4,3,2,0,1:T(8,128)(2,1)} %dynamic-slice_bitcast_fusion.10), channel_id=1, source_target_pairs={{0,4},{2,6},{4,0},{6,2},{8,12},{10,14},{12,8},{14,10},{16,20},{18,... | collective-permute-start | bytes 1572872 | tf_op jit(solution)/shard_map/ppermute | solution.py:709
  217.6 56.4 %collective-permute-start.14 = (bf16[2,2,2,2,32,1024]{5,4,0,1,2,3:T(8,128)(2,1)}, bf16[2,2,2,2,32,1024]{5,4,0,1,2,3:T(8,128)(2,1)}, u32[]{:S(2)}, u32[]{:S(2)}) collective-permute-start(bf16[2,2,2,2,32,1024]{5,4,0,1,2,3:T(8,128)(2,1)} %bitcast.289), channel_id=1, source_target_pairs={{0,2},{2,0},{4,6},{6,4},{8,10},{10,8},{12,14},{14,12},{16,18},{18,... | collective-permute-start | bytes 3145736 | tf_op jit(solution)/shard_map/ppermute | solution.py:709
  237.9 12.8 %collective-permute-start.20 = (bf16[1,64,2048]{2,1,0:T(8,128)(2,1)}, bf16[1,64,2048]{2,1,0:T(8,128)(2,1)}, u32[]{:S(2)}, u32[]{:S(2)}) collective-permute-start(bf16[1,64,2048]{2,1,0:T(8,128)(2,1)} %slice_select_fusion), channel_id=1, source_target_pairs={{0,1},{1,0},{2,3},{3,2},{4,5},{5,4},{6,7},{7,6},{8,9},{9,8},{10,11... | collective-permute-start | bytes 786440 | tf_op jit(solution)/shard_map/ppermute | solution.py:771
  250.7 23.3 %collective-permute-start.15 = (bf16[2,2,2,2,32,1024]{5,4,0,1,3,2:T(8,128)(2,1)}, bf16[2,2,2,2,32,1024]{5,4,0,1,3,2:T(8,128)(2,1)S(1)}, u32[]{:S(2)}, u32[]{:S(2)}) collective-permute-start(bf16[2,2,2,2,32,1024]{5,4,0,1,3,2:T(8,128)(2,1)} %bitcast.325), channel_id=1, source_target_pairs={{0,2},{2,0},{4,6},{6,4},{8,10},{10,8},{12,14},{14,12},{16,18},{18,... | collective-permute-start | bytes 3145736 | tf_op jit(solution)/shard_map/ppermute | solution.py:709
  254.5 5.4 %copy-start.31 = (bf16[2,2,2,32,1024]{4,3,2,0,1:T(8,128)(2,1)S(1)}, bf16[2,2,2,32,1024]{4,3,2,0,1:T(8,128)(2,1)}, u32[]{:S(2)}) copy-start(bf16[2,2,2,32,1024]{4,3,2,0,1:T(8,128)(2,1)} %dynamic-slice_bitcast_fusion.9) | copy-start | bytes 1572868
  259.9 14.2 %collective-permute-start.10 = (bf16[2,2,2,32,1024]{4,3,2,0,1:T(8,128)(2,1)S(1)}, bf16[2,2,2,32,1024]{4,3,2,0,1:T(8,128)(2,1)S(1)}, u32[]{:S(2)}, u32[]{:S(2)}) collective-permute-start(bf16[2,2,2,32,1024]{4,3,2,0,1:T(8,128)(2,1)S(1)} %copy-done.31), channel_id=1, source_target_pairs={{0,1},{1,0},{2,3},{3,2},{4,5},{5,4},{6,7},{7,6},{8,9},{9,8},{10,11... | collective-permute-start | bytes 1572872 | tf_op jit(solution)/shard_map/ppermute | solution.py:709
  273.3 53.4 %collective-permute-start.21 = (bf16[2,2,2,2,32,1024]{5,4,0,1,2,3:T(8,128)(2,1)}, bf16[2,2,2,2,32,1024]{5,4,0,1,2,3:T(8,128)(2,1)}, u32[]{:S(2)}, u32[]{:S(2)}) collective-permute-start(bf16[2,2,2,2,32,1024]{5,4,0,1,2,3:T(8,128)(2,1)} %bitcast.287), channel_id=1, source_target_pairs={{0,2},{2,0},{4,6},{6,4},{8,10},{10,8},{12,14},{14,12},{16,18},{18,... | collective-permute-start | bytes 3145736 | tf_op jit(solution)/shard_map/ppermute | solution.py:709
  273.3 3.9 copy-start.27
  273.3 53.4 %collective-permute-start.22 = (bf16[2,2,2,2,32,1024]{5,4,0,1,3,2:T(8,128)(2,1)}, bf16[2,2,2,2,32,1024]{5,4,0,1,3,2:T(8,128)(2,1)}, u32[]{:S(2)}, u32[]{:S(2)}) collective-permute-start(bf16[2,2,2,2,32,1024]{5,4,0,1,3,2:T(8,128)(2,1)} %bitcast.286), channel_id=1, source_target_pairs={{0,2},{2,0},{4,6},{6,4},{8,10},{10,8},{12,14},{14,12},{16,18},{18,... | collective-permute-start | bytes 3145736 | tf_op jit(solution)/shard_map/ppermute | solution.py:709
  274.0 3.2 copy-start.28
  274.1 3.1 copy-start.24
  274.1 3.7 copy-start
  276.2 3.2 copy-start.7
  277.2 28.4 %collective-permute-start.16 = (bf16[2,2,128,512]{3,2,0,1:T(8,128)(2,1)}, bf16[2,2,128,512]{3,2,0,1:T(8,128)(2,1)}, u32[]{:S(2)}, u32[]{:S(2)}) collective-permute-start(bf16[2,2,128,512]{3,2,0,1:T(8,128)(2,1)} %dynamic-slice_bitcast_fusion.8), channel_id=1, source_target_pairs={{0,4},{2,6},{4,0},{6,2},{8,12},{10,14},{12,8},{14,10},{16,20},{18,... | collective-permute-start | bytes 1572872 | tf_op jit(solution)/shard_map/ppermute | solution.py:709
  277.8 3.7 copy-start.2
  279.4 3.7 copy-start.9
  280.3 28.0 %collective-permute-start.17 = (bf16[2,2,128,512]{3,2,0,1:T(8,128)(2,1)}, bf16[2,2,128,512]{3,2,0,1:T(8,128)(2,1)}, u32[]{:S(2)}, u32[]{:S(2)}) collective-permute-start(bf16[2,2,128,512]{3,2,0,1:T(8,128)(2,1)} %dynamic-slice_bitcast_fusion.7), channel_id=1, source_target_pairs={{0,1},{1,0},{2,3},{3,2},{4,5},{5,4},{6,7},{7,6},{8,9},{9,8},{10,11... | collective-permute-start | bytes 1572872 | tf_op jit(solution)/shard_map/ppermute | solution.py:709
  284.0 25.9 %collective-permute-start.18 = (bf16[2,2,2,32,1024]{4,3,0,1,2:T(8,128)(2,1)}, bf16[2,2,2,32,1024]{4,3,0,1,2:T(8,128)(2,1)}, u32[]{:S(2)}, u32[]{:S(2)}) collective-permute-start(bf16[2,2,2,32,1024]{4,3,0,1,2:T(8,128)(2,1)} %dynamic-slice_bitcast_fusion.6), channel_id=1, source_target_pairs={{0,1},{1,0},{2,3},{3,2},{4,5},{5,4},{6,7},{7,6},{8,9},{9,8},{10,11... | collective-permute-start | bytes 1572872 | tf_op jit(solution)/shard_map/ppermute | solution.py:709
  284.9 17.4 %copy-start.5 = (bf16[2,2,2,2,32,1024]{5,4,3,0,1,2:T(8,128)(2,1)S(1)}, bf16[2,2,2,2,32,1024]{5,4,3,0,1,2:T(8,128)(2,1)}, u32[]{:S(2)}) copy-start(bf16[2,2,2,2,32,1024]{5,4,3,0,1,2:T(8,128)(2,1)} %copy-done.4) | copy-start | bytes 3145732
  300.8 2.8 copy-start.18
  300.8 2.8 copy-start.19
  305.6 13.0 %collective-permute-start.19 = (bf16[2,2,2,32,1024]{4,3,0,1,2:T(8,128)(2,1)S(1)}, bf16[2,2,2,32,1024]{4,3,0,1,2:T(8,128)(2,1)S(1)}, u32[]{:S(2)}, u32[]{:S(2)}) collective-permute-start(bf16[2,2,2,32,1024]{4,3,0,1,2:T(8,128)(2,1)S(1)} %dynamic-slice_bitcast_fusion.5), channel_id=1, source_target_pairs={{0,4},{2,6},{4,0},{6,2},{8,12},{10,14},{12,8},{14,10},{16,20},{18,... | collective-permute-start | bytes 1572872 | tf_op jit(solution)/shard_map/ppermute | solution.py:709
  307.2 19.5 %copy-start.32 = (f32[2,2,2,2,2,32,4]{5,4,3,2,1,0,6:T(2,128)}, f32[2,2,2,2,2,32,4]{5,4,3,2,1,0,6:T(2,128)S(1)}, u32[]{:S(2)}) copy-start(f32[2,2,2,2,2,32,4]{5,4,3,2,1,0,6:T(2,128)S(1)} %constant_dynamic-update-slice_fusion.1) | copy-start | bytes 49156
  308.3 18.5 %copy-start.12 = (bf16[2,2,2,2,32,1024]{5,4,0,1,2,3:T(8,128)(2,1)S(1)}, bf16[2,2,2,2,32,1024]{5,4,0,1,2,3:T(8,128)(2,1)}, u32[]{:S(2)}) copy-start(bf16[2,2,2,2,32,1024]{5,4,0,1,2,3:T(8,128)(2,1)} %copy-done.11) | copy-start | bytes 3145732
  308.3 51.1 %collective-permute-start.39 = (bf16[2,2,32,4096]{3,2,1,0:T(8,128)(2,1)}, bf16[2,2,32,4096]{3,2,1,0:T(8,128)(2,1)}, u32[]{:S(2)}, u32[]{:S(2)}) collective-permute-start(bf16[2,2,32,4096]{3,2,1,0:T(8,128)(2,1)} %dynamic-slice_bitcast_fusion), channel_id=1, source_target_pairs={{0,8},{2,10},{4,12},{6,14},{8,0},{10,2},{12,4},{14,6},{16,24},{18,... | collective-permute-start | bytes 3145736 | tf_op jit(solution)/shard_map/ppermute | solution.py:709
  326.7 3.0 copy-start.14
  326.8 80.6 %collective-permute-start.23 = (bf16[832,1024]{1,0:T(8,128)(2,1)}, bf16[832,1024]{1,0:T(8,128)(2,1)}, u32[]{:S(2)}, u32[]{:S(2)}) collective-permute-start(bf16[832,1024]{1,0:T(8,128)(2,1)} %feed_out.3), channel_id=1, source_target_pairs={{0,2},{2,0},{4,6},{6,4},{8,10},{10,8},{12,14},{14,12},{16,18},{18,... | collective-permute-start | bytes 5111816 | tf_op jit(solution)/shard_map/ppermute | solution.py:709
  328.2 12.2 %collective-permute-start.29 = (bf16[2,2,32,1024]{3,2,0,1:T(8,128)(2,1)S(1)}, bf16[2,2,32,1024]{3,2,0,1:T(8,128)(2,1)S(1)}, u32[]{:S(2)}, u32[]{:S(2)}) collective-permute-start(bf16[2,2,32,1024]{3,2,0,1:T(8,128)(2,1)S(1)} %dynamic-slice_bitcast_fusion.17), channel_id=1, source_target_pairs={{0,4},{2,6},{4,0},{6,2},{8,12},{10,14},{12,8},{14,10},{16,20},{18,... | collective-permute-start | bytes 786440 | tf_op jit(solution)/shard_map/ppermute | solution.py:709
  330.0 11.0 %collective-permute-start.30 = (bf16[2,2,32,1024]{3,2,0,1:T(8,128)(2,1)S(1)}, bf16[2,2,32,1024]{3,2,0,1:T(8,128)(2,1)S(1)}, u32[]{:S(2)}, u32[]{:S(2)}) collective-permute-start(bf16[2,2,32,1024]{3,2,0,1:T(8,128)(2,1)S(1)} %dynamic-slice_bitcast_fusion.16), channel_id=1, source_target_pairs={{0,1},{1,0},{2,3},{3,2},{4,5},{5,4},{6,7},{7,6},{8,9},{9,8},{10,11... | collective-permute-start | bytes 786440 | tf_op jit(solution)/shard_map/ppermute | solution.py:709
  331.0 3.7 copy-start.8
  333.6 3.9 copy-start.10
  333.6 19.1 %collective-permute-start.33 = (bf16[2,2,2,32,1024]{4,3,0,1,2:T(8,128)(2,1)}, bf16[2,2,2,32,1024]{4,3,0,1,2:T(8,128)(2,1)}, u32[]{:S(2)}, u32[]{:S(2)}) collective-permute-start(bf16[2,2,2,32,1024]{4,3,0,1,2:T(8,128)(2,1)} %dynamic-slice_bitcast_fusion.4), channel_id=1, source_target_pairs={{0,1},{1,0},{2,3},{3,2},{4,5},{5,4},{6,7},{7,6},{8,9},{9,8},{10,11... | collective-permute-start | bytes 1572872 | tf_op jit(solution)/shard_map/ppermute | solution.py:709
  340.4 16.2 %collective-permute-start.35 = (bf16[2,2,2,32,1024]{4,3,0,1,2:T(8,128)(2,1)}, bf16[2,2,2,32,1024]{4,3,0,1,2:T(8,128)(2,1)}, u32[]{:S(2)}, u32[]{:S(2)}) collective-permute-start(bf16[2,2,2,32,1024]{4,3,0,1,2:T(8,128)(2,1)} %dynamic-slice_bitcast_fusion.3), channel_id=1, source_target_pairs={{0,4},{2,6},{4,0},{6,2},{8,12},{10,14},{12,8},{14,10},{16,20},{18,... | collective-permute-start | bytes 1572872 | tf_op jit(solution)/shard_map/ppermute | solution.py:709
  341.8 10.3 %collective-permute-start.31 = (bf16[2,32,2048]{2,1,0:T(8,128)(2,1)}, bf16[2,32,2048]{2,1,0:T(8,128)(2,1)S(1)}, u32[]{:S(2)}, u32[]{:S(2)}) collective-permute-start(bf16[2,32,2048]{2,1,0:T(8,128)(2,1)} %fusion.38), channel_id=1, source_target_pairs={{0,8},{2,10},{4,12},{6,14},{8,0},{10,2},{12,4},{14,6},{16,24},{18,... | collective-permute-start | bytes 786440 | tf_op jit(solution)/shard_map/ppermute | solution.py:709
  352.1 15.9 %collective-permute-start.42 = (bf16[2,128,1024]{2,1,0:T(8,128)(2,1)}, bf16[2,128,1024]{2,1,0:T(8,128)(2,1)S(1)}, u32[]{:S(2)}, u32[]{:S(2)}) collective-permute-start(bf16[2,128,1024]{2,1,0:T(8,128)(2,1)} %fusion.23), channel_id=1, source_target_pairs={{0,8},{2,10},{4,12},{6,14},{8,0},{10,2},{12,4},{14,6},{16,24},{18,... | collective-permute-start | bytes 1572872 | tf_op jit(solution)/shard_map/ppermute | solution.py:709
  352.7 16.7 %collective-permute-start.32 = (bf16[32,2048]{1,0:T(8,128)(2,1)S(1)}, bf16[32,2048]{1,0:T(8,128)(2,1)S(1)}, u32[]{:S(2)}, u32[]{:S(2)}) collective-permute-start(bf16[32,2048]{1,0:T(8,128)(2,1)S(1)} %dynamic-slice_bitcast_fusion.19), channel_id=1, source_target_pairs={{0,16},{2,18},{4,20},{6,22},{8,24},{10,26},{12,28},{14,30},{16,0},... | collective-permute-start | bytes 393224 | tf_op jit(solution)/shard_map/ppermute | solution.py:709
  356.6 14.6 %collective-permute-start.34 = (bf16[2,2,32,1024]{3,2,0,1:T(8,128)(2,1)S(1)}, bf16[2,2,32,1024]{3,2,0,1:T(8,128)(2,1)S(1)}, u32[]{:S(2)}, u32[]{:S(2)}) collective-permute-start(bf16[2,2,32,1024]{3,2,0,1:T(8,128)(2,1)S(1)} %dynamic-slice_bitcast_fusion.15), channel_id=1, source_target_pairs={{0,4},{2,6},{4,0},{6,2},{8,12},{10,14},{12,8},{14,10},{16,20},{18,... | collective-permute-start | bytes 786440 | tf_op jit(solution)/shard_map/ppermute | solution.py:709
  359.5 11.9 %collective-permute-start.36 = (bf16[2,2,32,1024]{3,2,0,1:T(8,128)(2,1)S(1)}, bf16[2,2,32,1024]{3,2,0,1:T(8,128)(2,1)S(1)}, u32[]{:S(2)}, u32[]{:S(2)}) collective-permute-start(bf16[2,2,32,1024]{3,2,0,1:T(8,128)(2,1)S(1)} %dynamic-slice_bitcast_fusion.14), channel_id=1, source_target_pairs={{0,1},{1,0},{2,3},{3,2},{4,5},{5,4},{6,7},{7,6},{8,9},{9,8},{10,11... | collective-permute-start | bytes 786440 | tf_op jit(solution)/shard_map/ppermute | solution.py:709
  368.0 36.8 %collective-permute-start.40 = (bf16[2,32,4096]{2,1,0:T(8,128)(2,1)S(1)}, bf16[2,32,4096]{2,1,0:T(8,128)(2,1)S(1)}, u32[]{:S(2)}, u32[]{:S(2)}) collective-permute-start(bf16[2,32,4096]{2,1,0:T(8,128)(2,1)S(1)} %dynamic-slice_bitcast_fusion.2), channel_id=1, source_target_pairs={{0,16},{2,18},{4,20},{6,22},{8,24},{10,26},{12,28},{14,30},{16,0},... | collective-permute-start | bytes 1572872 | tf_op jit(solution)/shard_map/ppermute | solution.py:709
  369.4 34.3 %collective-permute-start.43 = (bf16[128,1024]{1,0:T(8,128)(2,1)S(1)}, bf16[128,1024]{1,0:T(8,128)(2,1)S(1)}, u32[]{:S(2)}, u32[]{:S(2)}) collective-permute-start(bf16[128,1024]{1,0:T(8,128)(2,1)S(1)} %dynamic-slice_bitcast_fusion.13), channel_id=1, source_target_pairs={{0,16},{2,18},{4,20},{6,22},{8,24},{10,26},{12,28},{14,30},{16,0},... | collective-permute-start | bytes 786440 | tf_op jit(solution)/shard_map/ppermute | solution.py:709
  371.5 33.1 %collective-permute-start.37 = (bf16[2,32,2048]{2,1,0:T(8,128)(2,1)S(1)}, bf16[2,32,2048]{2,1,0:T(8,128)(2,1)S(1)}, u32[]{:S(2)}, u32[]{:S(2)}) collective-permute-start(bf16[2,32,2048]{2,1,0:T(8,128)(2,1)S(1)} %fusion.34), channel_id=1, source_target_pairs={{0,8},{2,10},{4,12},{6,14},{8,0},{10,2},{12,4},{14,6},{16,24},{18,... | collective-permute-start | bytes 786440 | tf_op jit(solution)/shard_map/ppermute | solution.py:709
  404.7 10.9 %collective-permute-start.38 = (bf16[32,2048]{1,0:T(8,128)(2,1)S(1)}, bf16[32,2048]{1,0:T(8,128)(2,1)S(1)}, u32[]{:S(2)}, u32[]{:S(2)}) collective-permute-start(bf16[32,2048]{1,0:T(8,128)(2,1)S(1)} %dynamic-slice_bitcast_fusion.18), channel_id=1, source_target_pairs={{0,16},{2,18},{4,20},{6,22},{8,24},{10,26},{12,28},{14,30},{16,0},... | collective-permute-start | bytes 393224 | tf_op jit(solution)/shard_map/ppermute | solution.py:709
  407.3 7.7 %copy-start.33 = (f32[2,2,2,2,2,32,4]{5,4,3,2,1,0,6:T(2,128)S(1)}, f32[2,2,2,2,2,32,4]{5,4,3,2,1,0,6:T(2,128)}, u32[]{:S(2)}) copy-start(f32[2,2,2,2,2,32,4]{5,4,3,2,1,0,6:T(2,128)} %copy-done.32) | copy-start | bytes 49156
  407.3 14.6 %collective-permute-start.41 = (f32[32,4096]{1,0:T(8,128)S(1)}, f32[32,4096]{1,0:T(8,128)S(1)}, u32[]{:S(2)}, u32[]{:S(2)}) collective-permute-start(f32[32,4096]{1,0:T(8,128)S(1)} %dynamic-slice_bitcast_fusion.1), channel_id=1, source_target_pairs={{0,2},{2,0},{4,6},{6,4},{8,10},{10,8},{12,14},{14,12},{16,18},{18,... | collective-permute-start | bytes 1572872 | tf_op jit(solution)/shard_map/ppermute | solution.py:709
  415.0 1.4 collective-permute-start.24
  416.5 3.8 collective-permute-start.25
  420.3 3.7 collective-permute-start.26
  424.0 3.7 collective-permute-start.27
  427.7 6.2 %collective-permute-start.28 = (f32[32,4]{0,1:T(4,128)S(1)}, f32[32,4]{0,1:T(4,128)S(1)}, u32[]{:S(2)}, u32[]{:S(2)}) collective-permute-start(f32[32,4]{0,1:T(4,128)S(1)} %fusion.57), channel_id=1, source_target_pairs={{0,16},{2,18},{4,20},{6,22},{8,24},{10,26},{12,28},{14,30},{16,0},... | collective-permute-start | bytes 1544 | tf_op jit(solution)/shard_map/ppermute | solution.py:709
  (16 other events, 27.3 us)
